TPU v7x, 128 devices: a whole 4x4x4 slice. The times are simulated.
128 devices in a mesh: row: 8 (over z_lo, y), col: 16 (over x, z_hi, core).
Axes of the slice: x: 4, y: 4, z: 4 (z_hi: 2, z_lo: 2; z = z_hi * 2 + z_lo), core: 2. Of those that a mesh axis runs over, the one named last changes fastest.
Arguments:
- dst_embed: bfloat16 [16384, 64], P(('row', 'col')), may hold values from -24 to 24
- src_embed: bfloat16 [16384, 64], P(('row', 'col')), may hold values from -24 to 24
- series: bfloat16 [16384, 384], P(('row', 'col')), may hold values from -6 to 6
- w_self: bfloat16 [32, 32], replicated, may hold values from -1 to 1
- w_hop1: bfloat16 [32, 32], replicated, may hold values from -2.390625 to 2.390625
- w_hop2: bfloat16 [32, 32], replicated, may hold values from -9 to 9
- cotangent: bfloat16 [16384, 384], P(('row', 'col')), may hold values from -6 to 6
Outputs:
- output: bfloat16 [16384, 384], P(('row', 'col'))
- d_dst: float32 [16384, 64], P(('row', 'col'))
- d_src: float32 [16384, 64], P(('row', 'col'))
All inputs are finite; a program needn't handle non-finite values.
Results may differ from a plain program's by a relative error of at most 0.006.
Values may be sent and summed in bfloat16 or wider, within the bound.
No kernel may reach another device: no remote copies, remote signals or barrier semaphores. Data moves between devices by JAX's collectives and lax.ppermute only.
A program may use at most 128 MiB of HBM per device.

v0:
```python
import jax
import jax.numpy as jnp
from jax import lax
from jax.experimental import pallas as pl
from jax.experimental.pallas import tpu as pltpu
from jax.sharding import PartitionSpec as P

BF16 = jnp.bfloat16
F32 = jnp.float32
GROUP = 8
MIB = 1024 * 1024
VMEM_BYTES = 28 * MIB

SAME_CORE = [[2 * chip + core for chip in range(8)] for core in range(2)]
OTHER_CORE = [(i, i ^ 1) for i in range(16)]


def dot_nn(a, b):
    return lax.dot_general(a, b, (((1,), (0,)), ((), ())), preferred_element_type=F32)


def dot_nt(a, b):
    return lax.dot_general(a, b, (((1,), (1,)), ((), ())), preferred_element_type=F32)


def dot_tn(a, b):
    return lax.dot_general(a, b, (((0,), (0,)), ((), ())), preferred_element_type=F32)


def exchange_dst(blocks):
    return lax.all_to_all(blocks, "row", 0, 0)


def exchange_src(blocks):
    return lax.all_to_all(blocks, "col", 0, 0, axis_index_groups=SAME_CORE)


def swap_cores(blocks):
    return lax.ppermute(blocks, "col", OTHER_CORE)


def to_chip(blocks, x_step, z_step):
    pairs = []
    for i in range(16):
        x, z, core = i // 4, i // 2 % 2, i % 2
        pairs.append((i, (x + x_step) % 4 * 4 + (z + z_step) % 2 * 2 + core))
    return lax.ppermute(blocks, "col", pairs)


def gather_src(block):
    pair = jnp.stack([block, to_chip(block, 0, 1)])
    pairs = [pair] + [to_chip(pair, dx, 0) for dx in range(1, 4)]
    return jnp.concatenate(pairs), jnp.concatenate([swap_cores(p) for p in pairs])


def array(*shape, dtype=BF16):
    return jax.ShapeDtypeStruct(shape, dtype)


def whole(a):
    return pl.BlockSpec(a.shape, lambda *_: (0,) * len(a.shape))


def by_step(a):
    return pl.BlockSpec((a.shape[0] // 2,) + a.shape[1:], lambda i, *_: (i,) + (0,) * (len(a.shape) - 1))


def call(kernel, steps, ins, outs, scratch=(), flops=0, exps=0, kinds=None, vmem=VMEM_BYTES):
    kinds = kinds or {}
    sizes = [a.size * a.dtype.itemsize for a in list(ins) + list(outs)]
    specs = [kinds.get(i, whole)(a) for i, a in enumerate(list(ins) + list(outs))]
    return pl.pallas_call(
        kernel,
        grid=(steps,),
        in_specs=specs[: len(ins)],
        out_specs=specs[len(ins) :],
        out_shape=outs,
        scratch_shapes=scratch,
        compiler_params=pltpu.CompilerParams(vmem_limit_bytes=vmem),
        cost_estimate=pl.CostEstimate(flops=flops, bytes_accessed=sum(sizes), transcendentals=exps),
    )(*ins)


def at_step(step):
    return pl.when(pl.program_id(0) == step)


def pick(own_ref, other_ref):
    return jnp.where(pl.program_id(0) == 0, own_ref[...], other_ref[...])


def put(own_ref, other_ref, block, value):
    @at_step(0)
    def _():
        own_ref[block] = value

    @at_step(1)
    def _():
        other_ref[block] = value


def accumulate(total, part):
    @at_step(0)
    def _():
        total[...] = part

    @at_step(1)
    def _():
        total[...] += part


def side_by_side(blocks):
    return jnp.concatenate([blocks[b] for b in range(GROUP)], axis=1)


def nodes(block):
    return slice(128 * block, 128 * block + 128)


def series_of(packed):
    return jnp.concatenate([packed[b, 0:128, :] for b in range(GROUP)], axis=0)


def src_of(packed):
    pieces = [packed[:, 128:160, 0:128], packed[:, 128:160, 128:256]]
    return side_by_side(jnp.concatenate(pieces, axis=1))


def mixing(weight):
    size, chan = 384, weight.shape[0]
    place = lax.broadcasted_iota(jnp.int32, (size, chan), 0) % chan
    repeat = jnp.where(place == lax.broadcasted_iota(jnp.int32, (size, chan), 1), 1.0, 0.0).astype(BF16)
    tiled = dot_nt(dot_nn(repeat, weight).astype(BF16), repeat)
    rows = lax.broadcasted_iota(jnp.int32, (size, size), 0) // chan
    cols = lax.broadcasted_iota(jnp.int32, (size, size), 1) // chan
    return jnp.where(rows == cols, tiled, 0.0).astype(BF16)


def source_kernel(src_ref, series_ref, src_out):
    src_out[0:128, :] = series_ref[...]
    src_out[128:160, 0:128] = src_ref[0:32, :]
    src_out[128:160, 128:256] = src_ref[32:64, :]
    src_out[128:160, 256:384] = jnp.zeros((32, 128), BF16)


def prepare_kernel(
    dst_ref, series_ref, self_ref, hop1_ref, hop2_ref, cotangent_ref, dst_out, first_out, base_out, mix1_out, mix2_out
):
    mix1, mix2 = mixing(hop1_ref[...]), mixing(hop2_ref[...])
    cotangent = cotangent_ref[...]
    second = dot_nt(mix2, cotangent).astype(BF16)
    for block in range(GROUP):
        dst_out[block, 0:384, :] = second
        dst_out[block, 384:448, :] = dst_ref[...]
    first_out[...] = dot_nt(mix1, cotangent)
    base_out[...] = dot_nn(series_ref[...], mixing(self_ref[...]))
    mix1_out[...] = mix1
    mix2_out[...] = mix2


def prepare(*ins):
    outs = [
        array(GROUP, 448, 128),
        array(384, 128, dtype=F32),
        array(128, 384, dtype=F32),
        array(384, 384),
        array(384, 384),
    ]
    return call(prepare_kernel, 1, ins, outs, flops=3 * 2 * 128 * 384 * 384, vmem=60 * MIB)


def stats_kernel(own_ref, other_ref, dst_ref, out_ref, state, dst):
    @at_step(0)
    def _():
        state[...] = jnp.zeros_like(state)
        dst[...] = side_by_side(dst_ref[:, 384:448, :])

    lifted = jnp.maximum(dot_tn(src_of(pick(own_ref, other_ref)), dst[...]), 0.0)
    old = state[0:1, :]
    new = jnp.maximum(old, jnp.max(lifted, axis=0, keepdims=True))
    total = jnp.sum(jnp.exp(lifted - new), axis=0, keepdims=True)
    state[1:2, :] = state[1:2, :] * jnp.exp(old - new) + total
    state[0:1, :] = new

    @at_step(1)
    def _():
        out_ref[...] = jnp.broadcast_to(state[...][None], out_ref.shape)


def softmax_stats(own, other, dst):
    rows = dst.shape[0] * 128
    scratch = [pltpu.VMEM((2, rows), F32), pltpu.VMEM((64, rows), BF16)]
    outs = [array(GROUP, 2, rows, dtype=F32)]
    size = 2 * rows * rows
    return call(stats_kernel, 2, (own, other, dst), outs, scratch, 128 * size, size)[0]


def weights_of(src, dst, norm_ref):
    scores = dot_tn(src, dst)
    weights = jnp.exp(jnp.maximum(scores, 0.0) - norm_ref[0:1, :]) * norm_ref[1:2, :]
    return scores, weights


def hops_kernel(
    own_ref, other_ref, dst_ref, stats_ref, norm_ref, hop_ref, own_out, other_out, total, dst, second
):
    @at_step(0)
    def _():
        peak = stats_ref[0, 0:1, :]
        for d in range(1, GROUP):
            peak = jnp.maximum(peak, stats_ref[d, 0:1, :])
        row_sum = jnp.zeros_like(peak)
        for d in range(GROUP):
            row_sum += stats_ref[d, 1:2, :] * jnp.exp(stats_ref[d, 0:1, :] - peak)
        norm_ref[0:1, :] = peak
        norm_ref[1:2, :] = 1.0 / row_sum
        second[...] = side_by_side(dst_ref[:, 0:384, :])
        dst[...] = side_by_side(dst_ref[:, 384:448, :])

    packed = pick(own_ref, other_ref)
    adjacency = weights_of(src_of(packed), dst[...], norm_ref)[1].astype(BF16)
    carried = dot_nt(second[...], adjacency).astype(BF16)
    for block in range(GROUP):
        put(own_out, other_out, block, carried[:, nodes(block)])
    accumulate(total, dot_tn(series_of(packed), adjacency))

    @at_step(1)
    def _():
        for block in range(GROUP):
            hop_ref[block] = total[:, nodes(block)].astype(BF16)


def first_hops(own, other, dst, stats):
    rows = dst.shape[0] * 128
    outs = [array(2, rows, dtype=F32)] + [array(GROUP, 384, 128)] * 3
    scratch = [pltpu.VMEM((384, rows), F32), pltpu.VMEM((64, rows), BF16), pltpu.VMEM((384, rows), BF16)]
    size = 2 * rows * rows
    return call(hops_kernel, 2, (own, other, dst, stats), outs, scratch, 2 * 832 * size, size)


def sum_of(pack_ref, start, stop):
    total = pack_ref[0, start:stop, :].astype(F32)
    for d in range(1, GROUP):
        total += pack_ref[d, start:stop, :].astype(F32)
    return total


def cores_kernel(own_ref, other_ref, *outs):
    for place, out in enumerate(outs):
        pair = slice(2 * place, 2 * place + 2)
        out[...] = (own_ref[pair].astype(F32) + other_ref[pair].astype(F32)).astype(BF16)


def join_kernel(hop_ref, a_ref, b_ref, c_ref, d_ref, hop_out, mine_out, other_out):
    def total(place):
        parts = [ref[place].astype(F32) for ref in (a_ref, b_ref, c_ref, d_ref)]
        return (parts[0] + parts[1]) + (parts[2] + parts[3])

    other_out[...] = total(1).astype(BF16)
    hop_out[...] = sum_of(hop_ref, 0, 384).T.astype(BF16)
    mine_out[...] = total(0)


def first_grad_kernel(mixed_ref, mine_ref, other_ref, out_ref):
    grad = (mixed_ref[...] + (mine_ref[...] + other_ref[...].astype(F32))).astype(BF16)
    for block in range(GROUP):
        out_ref[block] = grad


def three_terms(value):
    high = value.astype(BF16).astype(F32)
    middle = (value - high).astype(BF16).astype(F32)
    return [high, middle, value - high - middle]


SECOND, ABOVE, BELOW, INNER, SHIFT, LAST = 0, 384, 448, 512, 536, 544


def grad_kernel(
    own_ref, other_ref, hop_own_ref, hop_other_ref, dst_ref, norm_ref, first_ref,
    pack_ref, shift_ref, own_out, other_out, inner, mass, above, below, dst, grads, adj, wide, second,
):
    step = pl.program_id(0)
    half = step % 2

    @at_step(0)
    def _():
        dst[...] = side_by_side(dst_ref[:, 384:448, :])
        grads[0:384, :] = side_by_side(dst_ref[:, 0:384, :])
        grads[384:768, :] = side_by_side(first_ref)

    packed = jnp.where(half == 0, own_ref[...], other_ref[...])
    src = src_of(packed)

    @pl.when(step < 2)
    def _():
        scores, weights = weights_of(src, dst[...], norm_ref)
        hop = jnp.where(half == 0, hop_own_ref[...], hop_other_ref[...])
        adj_grad = dot_nn(jnp.concatenate([hop, series_of(packed)], axis=1), grads[...])
        adj[half] = adj_grad
        wide[half] = jnp.where(scores > 0.0, weights, 0.0)
        hop_part = dot_tn(hop, weights.astype(BF16))
        second[...] = jnp.where(step == 0, hop_part, second[...] + hop_part)
        total = jnp.sum(weights * adj_grad, axis=0, keepdims=True)
        weight = jnp.sum(weights, axis=0, keepdims=True)
        inner[...] = jnp.where(step == 0, total, inner[...] + total)
        mass[...] = jnp.where(step == 0, weight, mass[...] + weight)

    @pl.when(step >= 2)
    def _():
        shift = jnp.where(mass[...] > 1e-30, inner[...] / jnp.maximum(mass[...], 1e-30), 0.0)
        masked = wide[half]
        graded = (masked * (adj[half] - shift)).astype(BF16)
        masked = masked.astype(BF16)
        up, low = dot_nn(src, graded), dot_nn(src, masked)
        above[...] = jnp.where(step == 2, up, above[...] + up)
        below[...] = jnp.where(step == 2, low, below[...] + low)
        d_src = dot_nt(dst[...], graded)

        @pl.when(half == 0)
        def _():
            for block in range(GROUP):
                own_out[block] = d_src[:, nodes(block)]

        @pl.when(half == 1)
        def _():
            shift_ref[...] = shift
            for block in range(GROUP):
                other_out[block] = d_src[:, nodes(block)]
            sums = [term[:, nodes(block)] for term in three_terms(inner[...]) for block in range(GROUP)]
            sums = jnp.concatenate(sums, axis=0)
            shifts = jnp.concatenate(three_terms(shift), axis=0)
            for block in range(GROUP):
                tail = jnp.concatenate([sums, shifts[:, nodes(block)], jnp.zeros((5, 128), F32)], axis=0)
                pack_ref[block, SECOND:ABOVE, :] = second[:, nodes(block)].astype(BF16)
                pack_ref[block, ABOVE:BELOW, :] = above[:, nodes(block)].astype(BF16)
                pack_ref[block, BELOW:INNER, :] = below[:, nodes(block)].astype(BF16)
                pack_ref[block, INNER:LAST, :] = tail.astype(BF16)


def embed_grads(*ins):
    rows = ins[4].shape[0] * 128
    outs = [
        array(GROUP, LAST, 128),
        array(1, rows, dtype=F32),
        array(GROUP, 64, 128, dtype=F32),
        array(GROUP, 64, 128, dtype=F32),
    ]
    scratch = [
        pltpu.VMEM((1, rows), F32),
        pltpu.VMEM((1, rows), F32),
        pltpu.VMEM((64, rows), F32),
        pltpu.VMEM((64, rows), F32),
        pltpu.VMEM((64, rows), BF16),
        pltpu.VMEM((768, rows), BF16),
        pltpu.VMEM((2, rows, rows), F32),
        pltpu.VMEM((2, rows, rows), F32),
        pltpu.VMEM((384, rows), F32),
    ]

    size = 2 * rows * rows
    return call(
        grad_kernel, 4, ins, outs, scratch, 2 * 1408 * size, size, vmem=46 * MIB
    )


def inner_of(pack_ref):
    terms = sum_of(pack_ref, INNER, LAST)
    return terms[0:8] + (terms[8:16] + terms[16:24])


def src_kernel(
    own_ref, other_ref, dst_ref, norm_ref, pack_ref, shift_ref, own_part, other_part, own_out, other_out, scaled, dst
):
    @at_step(0)
    def _():
        dst[...] = side_by_side(dst_ref[:, 384:448, :])
        inner = inner_of(pack_ref)
        for block in range(GROUP):
            change = shift_ref[:, nodes(block)] - inner[block : block + 1, :]
            scaled[:, nodes(block)] = (dst[:, nodes(block)].astype(F32) * change).astype(BF16)

    scores, weights = weights_of(src_of(pick(own_ref, other_ref)), dst[...], norm_ref)
    part = dot_nt(scaled[...], jnp.where(scores > 0.0, weights, 0.0).astype(BF16))

    me = lax.axis_index("col")
    for block in range(GROUP):
        place = (me // 4 + 4 - block // 2) % 4 * 2 + (me // 2 + block) % 2

        @at_step(0)
        def _(block=block, place=place):
            own_out[place] = own_part[block] + part[:, nodes(block)]

        @at_step(1)
        def _(block=block, place=place):
            other_out[place] = other_part[block] + part[:, nodes(block)]


def src_grads(*ins):
    rows = ins[2].shape[0] * 128
    outs = [array(GROUP, 64, 128, dtype=F32), array(GROUP, 64, 128, dtype=F32)]
    scratch = [pltpu.VMEM((64, rows), BF16), pltpu.VMEM((64, rows), BF16)]
    size = 2 * rows * rows
    return call(src_kernel, 2, ins, outs, scratch, 256 * size, size)


def output_kernel(pack_ref, hop_ref, base_ref, mix1_ref, mix2_ref, out_ref, d_dst_ref):
    second = sum_of(pack_ref, SECOND, ABOVE).T.astype(BF16)
    mixed = base_ref[...] + dot_nn(hop_ref[...], mix1_ref[...]) + dot_nn(second, mix2_ref[...])
    out_ref[...] = mixed.astype(BF16)
    me = lax.axis_index("row")
    inner = inner_of(pack_ref)
    places = lax.broadcasted_iota(jnp.int32, inner.shape, 0)
    inner = jnp.sum(jnp.where(places == me, inner, 0.0), axis=0, keepdims=True)
    d_dst = jnp.zeros((64, 128), F32)
    for d in range(GROUP):
        tail = pack_ref[d, INNER:LAST, :].astype(F32)
        shift = tail[24:25] + (tail[25:26] + tail[26:27])
        above, below = pack_ref[d, ABOVE:BELOW, :].astype(F32), pack_ref[d, BELOW:INNER, :].astype(F32)
        d_dst += above + (shift - inner) * below
    d_dst_ref[...] = d_dst


def local(dst_embed, src_embed, series, w_self, w_hop1, w_hop2, cotangent):
    src = call(source_kernel, 1, (src_embed.T, series), [array(160, 384)], vmem=60 * MIB)[0]
    src_own, src_other = gather_src(src)
    dst, first_mixed, base, mix1, mix2 = prepare(dst_embed.T, series, w_self, w_hop1, w_hop2, cotangent)
    dst = exchange_dst(dst)
    stats = exchange_dst(softmax_stats(src_own, src_other, dst))

    norm, hop, own, other = first_hops(src_own, src_other, dst, stats)
    hop = exchange_dst(hop)
    pairs = call(cores_kernel, 1, (own, swap_cores(other)), [array(2, 384, 128)] * 4)
    pairs = [pairs[0]] + [to_chip(pairs[dx], -dx, 0) for dx in range(1, 4)]
    hop, mine, rest = call(
        join_kernel, 1, (hop, *pairs), [array(128, 384), array(384, 128, dtype=F32), array(384, 128)]
    )
    rest = to_chip(rest, 0, 1)
    first = call(first_grad_kernel, 1, (first_mixed, mine, rest), [array(GROUP, 384, 128)])[0]
    first = exchange_dst(first)
    hop_own, hop_other = (half.reshape(-1, 384) for half in gather_src(hop))

    pack, shift, own, other = embed_grads(src_own, src_other, hop_own, hop_other, dst, norm, first)
    pack = exchange_dst(pack)
    own, other = src_grads(src_own, src_other, dst, norm, pack, shift, own, other)
    output, d_dst = call(
        output_kernel, 1, (pack, hop, base, mix1, mix2), [array(128, 384), array(64, 128, dtype=F32)],
        flops=4 * 128 * 384 * 384,
    )
    d_src = jnp.sum(exchange_src(own + swap_cores(other)), axis=0)
    return output, d_dst.T, d_src.T


def solution(mesh):
    blocks = P(("row", "col"), None)
    return jax.shard_map(
        local,
        mesh=mesh,
        in_specs=(blocks, blocks, blocks, P(), P(), P(), blocks),
        out_specs=(blocks, blocks, blocks),
        check_vma=False,
    )
```

profile of v0, /device:TPU:0, one launch (start us, length us, event | category | flops | bytes accessed | tf_op | source)
XLA Modules:
  0.0 162.4 jit_solution(2714066261175165561)
XLA Ops:
  2.2 4.0 %collective-permute-start = (bf16[160,384]{1,0:T(8,128)(2,1)}, bf16[160,384]{1,0:T(8,128)(2,1)S(1)}, u32[]{:S(2)}, u32[]{:S(2)}) collective-permute-start(bf16[160,384]{1,0:T(8,128)(2,1)} %shard_map.94), channel_id=1, source_target_pairs={{0,2},{1,3},{2,0},{3,1},{4,6},{5,7},{6,4},{7,5},{8,10},{9,11},{10,... | collective-permute-start | bytes 368648 | tf_op jit(solution)/shard_map/ppermute | solution.py:47
  6.2 3.3 %shard_map.95 = (bf16[8,448,128]{2,1,0:T(8,128)(2,1)}, f32[384,128]{1,0:T(8,128)}, f32[128,384]{1,0:T(8,128)}, bf16[384,384]{1,0:T(8,128)(2,1)}, bf16[384,384]{1,0:T(8,128)(2,1)}) custom-call(bf16[64,128]{1,0:T(8,128)(2,1)} %bitcast.22, bf16[128,384]{1,0:T(8,128)(2,1)} %series_ref.3, bf16[32,32]{1,0:T(8,128)(2,1)} %self_ref.1, bf16[32,32]{1,0:T(8,128)(2,1)} %hop1_ref.1, ...), custom_call_target="tpu_custom_call" | custom-call | flops 113246208 | bytes 2119680 | tf_op jit(solution)/shard_map/pallas_call | solution.py:72
  9.4 4.9 %all-to-all-start = ((bf16[8,448,128]{2,1,0:T(8,128)(2,1)}), bf16[8,448,128]{2,1,0:T(8,128)(2,1)S(1)}, u32[]{:S(2)}, u32[]{:S(2)}) async-start(bf16[8,448,128]{2,1,0:T(8,128)(2,1)} %get-tuple-element.27), calls=%async_computation | async-start | bytes 1835008 | tf_op jit(solution)/shard_map/all_to_all | solution.py:31
  14.5 2.8 %collective-permute-start.3 = (bf16[2,160,384]{2,1,0:T(8,128)(2,1)S(1)}, bf16[2,160,384]{2,1,0:T(8,128)(2,1)S(1)}, u32[]{:S(2)}, u32[]{:S(2)}) collective-permute-start(bf16[2,160,384]{2,1,0:T(8,128)(2,1)S(1)} %pad_maximum_fusion.1), channel_id=1, source_target_pairs={{0,12},{1,13},{2,14},{3,15},{4,0},{5,1},{6,2},{7,3},{8,4},{9,5},{1... | collective-permute-start | bytes 737288 | tf_op jit(solution)/shard_map/ppermute | solution.py:47
  19.1 9.4 %collective-permute-done.3 = bf16[2,160,384]{2,1,0:T(8,128)(2,1)S(1)} collective-permute-done((bf16[2,160,384]{2,1,0:T(8,128)(2,1)S(1)}, bf16[2,160,384]{2,1,0:T(8,128)(2,1)S(1)}, u32[]{:S(2)}, u32[]{:S(2)}) %collective-permute-start.3) | collective-permute-done | bytes 245792 | tf_op jit(solution)/shard_map/ppermute | solution.py:47
  29.0 3.2 %collective-permute-done.1 = bf16[2,160,384]{2,1,0:T(8,128)(2,1)S(1)} collective-permute-done((bf16[2,160,384]{2,1,0:T(8,128)(2,1)S(1)}, bf16[2,160,384]{2,1,0:T(8,128)(2,1)S(1)}, u32[]{:S(2)}, u32[]{:S(2)}) %collective-permute-start.1) | collective-permute-done | bytes 245792 | tf_op jit(solution)/shard_map/ppermute | solution.py:47
  33.8 3.0 %shard_map.96 = f32[8,2,1024]{2,1,0:T(2,128)S(1)} custom-call(bf16[8,160,384]{2,1,0:T(8,128)(2,1)S(1)} %constant_dynamic-update-slice_fusion.own_ref, bf16[8,160,384]{2,1,0:T(8,128)(2,1)S(1)} %constant_dynamic-update-slice_fusion.5.other_ref, bf16[8,448,128]{2,1,0:T(8,128)(2,1)S(1)} %all-to-all-done.dst_ref), custom_call_target="tpu_custom_call" | custom-call | flops 268435456 | bytes 2949120 | tf_op jit(solution)/shard_map/pallas_call | solution.py:72
  36.8 11.8 %all_to_all.30.stats_ref = f32[8,2,1024]{2,1,0:T(2,128)S(1)} all-to-all(f32[8,2,1024]{2,1,0:T(2,128)S(1)} %shard_map.96), channel_id=1, replica_groups=mesh['row'=8,'col'=16] {'row'}, dimensions={0} | all-to-all | bytes 131072 | tf_op jit(solution)/shard_map/all_to_all | solution.py:31
  48.7 7.1 %shard_map.97 = (f32[2,1024]{1,0:T(2,128)S(1)}, bf16[8,384,128]{2,1,0:T(8,128)(2,1)S(1)}, bf16[8,384,128]{2,1,0:T(8,128)(2,1)S(1)}, bf16[8,384,128]{2,1,0:T(8,128)(2,1)}) custom-call(bf16[8,160,384]{2,1,0:T(8,128)(2,1)S(1)} %constant_dynamic-update-slice_fusion.own_ref, bf16[8,160,384]{2,1,0:T(8,128)(2,1)S(1)} %constant_dynamic-update-slice_fusion.5.other_ref, ...), custom_call_target="tpu_custom_call" | custom-call | flops 3489660928 | bytes 5316608 | tf_op jit(solution)/shard_map/pallas_call | solution.py:72
  57.6 3.5 %all-to-all-start.2 = ((bf16[8,384,128]{2,1,0:T(8,128)(2,1)}), bf16[8,384,128]{2,1,0:T(8,128)(2,1)S(1)}, u32[]{:S(2)}, u32[]{:S(2)}) async-start(bf16[8,384,128]{2,1,0:T(8,128)(2,1)} %copy-done.3), calls=%async_computation.2 | async-start | bytes 1572864 | tf_op jit(solution)/shard_map/all_to_all | solution.py:31
  62.3 2.0 %shard_map.98 = (bf16[2,384,128]{2,1,0:T(8,128)(2,1)S(1)}, bf16[2,384,128]{2,1,0:T(8,128)(2,1)}, bf16[2,384,128]{2,1,0:T(8,128)(2,1)}, bf16[2,384,128]{2,1,0:T(8,128)(2,1)}) custom-call(bf16[8,384,128]{2,1,0:T(8,128)(2,1)S(1)} %copy-done.5, bf16[8,384,128]{2,1,0:T(8,128)(2,1)} %collective-permute-done.8.other_ref), custom_call_target="tpu_custom_call" | custom-call | bytes 2359296 | tf_op jit(solution)/shard_map/pallas_call | solution.py:72
  66.5 8.4 %all-to-all-done.2.hop_ref = bf16[8,384,128]{2,1,0:T(8,128)(2,1)S(1)} async-done(((bf16[8,384,128]{2,1,0:T(8,128)(2,1)}), bf16[8,384,128]{2,1,0:T(8,128)(2,1)S(1)}, u32[]{:S(2)}, u32[]{:S(2)}) %all-to-all-start.2) | async-done | bytes 786464 | tf_op jit(solution)/shard_map/all_to_all | solution.py:31
  74.9 3.1 %collective-permute-done.11.d_ref = bf16[2,384,128]{2,1,0:T(8,128)(2,1)} collective-permute-done((bf16[2,384,128]{2,1,0:T(8,128)(2,1)}, bf16[2,384,128]{2,1,0:T(8,128)(2,1)}, u32[]{:S(2)}, u32[]{:S(2)}) %collective-permute-start.11) | collective-permute-done | bytes 196640 | tf_op jit(solution)/shard_map/ppermute | solution.py:47
  81.3 2.4 %collective-permute-start.20 = (bf16[384,128]{1,0:T(8,128)(2,1)S(1)}, bf16[384,128]{1,0:T(8,128)(2,1)S(1)}, u32[]{:S(2)}, u32[]{:S(2)}) collective-permute-start(bf16[384,128]{1,0:T(8,128)(2,1)S(1)} %get-tuple-element.39), channel_id=1, source_target_pairs={{0,2},{1,3},{2,0},{3,1},{4,6},{5,7},{6,4},{7,5},{8,10},{9,11},{10,... | collective-permute-start | bytes 294920 | tf_op jit(solution)/shard_map/ppermute | solution.py:47
  83.6 2.7 %collective-permute-done.12 = bf16[128,384]{1,0:T(8,128)(2,1)S(1)} collective-permute-done((bf16[128,384]{1,0:T(8,128)(2,1)S(1)}, bf16[128,384]{1,0:T(8,128)(2,1)S(1)}, u32[]{:S(2)}, u32[]{:S(2)}) %collective-permute-start.12) | collective-permute-done | bytes 98336 | tf_op jit(solution)/shard_map/ppermute | solution.py:47
  89.6 5.6 %all-to-all-start.3 = ((bf16[8,384,128]{2,1,0:T(8,128)(2,1)}), bf16[8,384,128]{2,1,0:T(8,128)(2,1)}, u32[]{:S(2)}, u32[]{:S(2)}) async-start(bf16[8,384,128]{2,1,0:T(8,128)(2,1)} %shard_map.100), calls=%async_computation.3 | async-start | bytes 1572864 | tf_op jit(solution)/shard_map/all_to_all | solution.py:31
  96.7 3.4 %collective-permute-done.13 = bf16[2,128,384]{2,1,0:T(8,128)(2,1)} collective-permute-done((bf16[2,128,384]{2,1,0:T(8,128)(2,1)S(1)}, bf16[2,128,384]{2,1,0:T(8,128)(2,1)}, u32[]{:S(2)}, u32[]{:S(2)}) %collective-permute-start.13) | collective-permute-done | bytes 196640 | tf_op jit(solution)/shard_map/ppermute | solution.py:47
  101.8 1.7 %constant_dynamic-update-slice_fusion.10 = bf16[8,128,384]{2,1,0:T(8,128)(2,1)} fusion(bf16[8,128,384]{2,1,0:T(8,128)(2,1)} %constant_dynamic-update-slice_fusion.11, bf16[2,128,384]{2,1,0:T(8,128)(2,1)} %collective-permute-done.14), kind=kLoop, calls=%fused_computation.13 | loop fusion | bytes 393216
  106.1 2.0 %all-to-all-done.3.first_ref = bf16[8,384,128]{2,1,0:T(8,128)(2,1)} async-done(((bf16[8,384,128]{2,1,0:T(8,128)(2,1)}), bf16[8,384,128]{2,1,0:T(8,128)(2,1)}, u32[]{:S(2)}, u32[]{:S(2)}) %all-to-all-start.3) | async-done | bytes 786464 | tf_op jit(solution)/shard_map/all_to_all | solution.py:31
  109.3 13.2 %shard_map.101 = (bf16[8,544,128]{2,1,0:T(8,128)(2,1)S(1)}, f32[1,1024]{1,0:T(1,128)S(1)}, f32[8,64,128]{2,1,0:T(8,128)S(1)}, f32[8,64,128]{2,1,0:T(8,128)S(1)}) custom-call(bf16[8,160,384]{2,1,0:T(8,128)(2,1)S(1)} %copy-done.1, bf16[8,160,384]{2,1,0:T(8,128)(2,1)S(1)} %constant_dynamic-update-slice_fusion.5.other_ref, ...), custom_call_target="tpu_custom_call" | custom-call | flops 5905580032 | bytes 6893568 | tf_op jit(solution)/shard_map/pallas_call | solution.py:72
  122.6 20.2 %all_to_all.31.pack_ref = bf16[8,544,128]{2,1,0:T(8,128)(2,1)S(1)} all-to-all(bf16[8,544,128]{2,1,0:T(8,128)(2,1)S(1)} %get-tuple-element.40), channel_id=1, replica_groups=mesh['row'=8,'col'=16] {'row'}, dimensions={0} | all-to-all | bytes 2228224 | tf_op jit(solution)/shard_map/all_to_all | solution.py:31
  142.7 3.6 %shard_map.103 = (f32[8,64,128]{2,1,0:T(8,128)S(1)}, f32[8,64,128]{2,1,0:T(8,128)S(1)}) custom-call(bf16[8,160,384]{2,1,0:T(8,128)(2,1)S(1)} %copy-done.2, bf16[8,160,384]{2,1,0:T(8,128)(2,1)S(1)} %constant_dynamic-update-slice_fusion.5.other_ref, bf16[8,448,128]{2,1,0:T(8,128)(2,1)S(1)} %all-to-all-done.dst_ref, f32[2,1024]{1,0:T(2,128)S(1)} %get-tuple-element.36.norm_ref, ...), custom_call_target="tpu_custom_call" | custom-call | flops 536870912 | bytes 5058560 | tf_op jit(solution)/shard_map/pallas_call | solution.py:72
  148.8 4.2 %all-to-all-start.5 = ((f32[8,64,128]{2,1,0:T(8,128)}), f32[8,64,128]{2,1,0:T(8,128)S(1)}, u32[]{:S(2)}, u32[]{:S(2)}) async-start(f32[8,64,128]{2,1,0:T(8,128)} %add.3), calls=%async_computation.5 | async-start | bytes 524288 | tf_op jit(solution)/shard_map/all_to_all | solution.py:35
  154.0 7.8 %all-to-all-done.5 = f32[8,64,128]{2,1,0:T(8,128)S(1)} async-done(((f32[8,64,128]{2,1,0:T(8,128)}), f32[8,64,128]{2,1,0:T(8,128)S(1)}, u32[]{:S(2)}, u32[]{:S(2)}) %all-to-all-start.5) | async-done | bytes 262176 | tf_op jit(solution)/shard_map/all_to_all | solution.py:35
  (83 shorter events, 28.0 us)
Async XLA Ops:
  2.2 12.2 %collective-permute-start = (bf16[160,384]{1,0:T(8,128)(2,1)}, bf16[160,384]{1,0:T(8,128)(2,1)S(1)}, u32[]{:S(2)}, u32[]{:S(2)}) collective-permute-start(bf16[160,384]{1,0:T(8,128)(2,1)} %shard_map.94), channel_id=1, source_target_pairs={{0,2},{1,3},{2,0},{3,1},{4,6},{5,7},{6,4},{7,5},{8,10},{9,11},{10,... | collective-permute-start | bytes 368648 | tf_op jit(solution)/shard_map/ppermute | solution.py:47
  9.4 24.4 %all-to-all-start = ((bf16[8,448,128]{2,1,0:T(8,128)(2,1)}), bf16[8,448,128]{2,1,0:T(8,128)(2,1)S(1)}, u32[]{:S(2)}, u32[]{:S(2)}) async-start(bf16[8,448,128]{2,1,0:T(8,128)(2,1)} %get-tuple-element.27), calls=%async_computation | async-start | bytes 1835008 | tf_op jit(solution)/shard_map/all_to_all | solution.py:31
  14.4 17.7 %collective-permute-start.4 = (bf16[2,160,384]{2,1,0:T(8,128)(2,1)S(1)}, bf16[2,160,384]{2,1,0:T(8,128)(2,1)S(1)}, u32[]{:S(2)}, u32[]{:S(2)}) collective-permute-start(bf16[2,160,384]{2,1,0:T(8,128)(2,1)S(1)} %pad_maximum_fusion.1), channel_id=1, source_target_pairs={{0,1},{1,0},{2,3},{3,2},{4,5},{5,4},{6,7},{7,6},{8,9},{9,8},{10,11... | collective-permute-start | bytes 737288 | tf_op jit(solution)/shard_map/ppermute | solution.py:39
  14.5 13.9 %collective-permute-start.3 = (bf16[2,160,384]{2,1,0:T(8,128)(2,1)S(1)}, bf16[2,160,384]{2,1,0:T(8,128)(2,1)S(1)}, u32[]{:S(2)}, u32[]{:S(2)}) collective-permute-start(bf16[2,160,384]{2,1,0:T(8,128)(2,1)S(1)} %pad_maximum_fusion.1), channel_id=1, source_target_pairs={{0,12},{1,13},{2,14},{3,15},{4,0},{5,1},{6,2},{7,3},{8,4},{9,5},{1... | collective-permute-start | bytes 737288 | tf_op jit(solution)/shard_map/ppermute | solution.py:47
  17.3 11.1 %collective-permute-start.2 = (bf16[2,160,384]{2,1,0:T(8,128)(2,1)S(1)}, bf16[2,160,384]{2,1,0:T(8,128)(2,1)S(1)}, u32[]{:S(2)}, u32[]{:S(2)}) collective-permute-start(bf16[2,160,384]{2,1,0:T(8,128)(2,1)S(1)} %pad_maximum_fusion.1), channel_id=1, source_target_pairs={{0,8},{1,9},{2,10},{3,11},{4,12},{5,13},{6,14},{7,15},{8,0},{9,1},... | collective-permute-start | bytes 737288 | tf_op jit(solution)/shard_map/ppermute | solution.py:47
  18.1 14.0 %collective-permute-start.1 = (bf16[2,160,384]{2,1,0:T(8,128)(2,1)S(1)}, bf16[2,160,384]{2,1,0:T(8,128)(2,1)S(1)}, u32[]{:S(2)}, u32[]{:S(2)}) collective-permute-start(bf16[2,160,384]{2,1,0:T(8,128)(2,1)S(1)} %pad_maximum_fusion.1), channel_id=1, source_target_pairs={{0,4},{1,5},{2,6},{3,7},{4,8},{5,9},{6,10},{7,11},{8,12},{9,13},{1... | collective-permute-start | bytes 737288 | tf_op jit(solution)/shard_map/ppermute | solution.py:47
  28.4 5.3 %collective-permute-start.7 = (bf16[2,160,384]{2,1,0:T(8,128)(2,1)S(1)}, bf16[2,160,384]{2,1,0:T(8,128)(2,1)S(1)}, u32[]{:S(2)}, u32[]{:S(2)}) collective-permute-start(bf16[2,160,384]{2,1,0:T(8,128)(2,1)S(1)} %collective-permute-done.3), channel_id=1, source_target_pairs={{0,1},{1,0},{2,3},{3,2},{4,5},{5,4},{6,7},{7,6},{8,9},{9,8},{10,11... | collective-permute-start | bytes 737288 | tf_op jit(solution)/shard_map/ppermute | solution.py:39
  28.5 5.2 %collective-permute-start.6 = (bf16[2,160,384]{2,1,0:T(8,128)(2,1)S(1)}, bf16[2,160,384]{2,1,0:T(8,128)(2,1)S(1)}, u32[]{:S(2)}, u32[]{:S(2)}) collective-permute-start(bf16[2,160,384]{2,1,0:T(8,128)(2,1)S(1)} %collective-permute-done.2), channel_id=1, source_target_pairs={{0,1},{1,0},{2,3},{3,2},{4,5},{5,4},{6,7},{7,6},{8,9},{9,8},{10,11... | collective-permute-start | bytes 737288 | tf_op jit(solution)/shard_map/ppermute | solution.py:39
  57.6 3.6 %collective-permute-start.8 = (bf16[8,384,128]{2,1,0:T(8,128)(2,1)}, bf16[8,384,128]{2,1,0:T(8,128)(2,1)}, u32[]{:S(2)}, u32[]{:S(2)}) collective-permute-start(bf16[8,384,128]{2,1,0:T(8,128)(2,1)} %get-tuple-element.30), channel_id=1, source_target_pairs={{0,1},{1,0},{2,3},{3,2},{4,5},{5,4},{6,7},{7,6},{8,9},{9,8},{10,11... | collective-permute-start | bytes 2359304 | tf_op jit(solution)/shard_map/ppermute | solution.py:39
  57.6 17.3 %all-to-all-start.2 = ((bf16[8,384,128]{2,1,0:T(8,128)(2,1)}), bf16[8,384,128]{2,1,0:T(8,128)(2,1)S(1)}, u32[]{:S(2)}, u32[]{:S(2)}) async-start(bf16[8,384,128]{2,1,0:T(8,128)(2,1)} %copy-done.3), calls=%async_computation.2 | async-start | bytes 1572864 | tf_op jit(solution)/shard_map/all_to_all | solution.py:31
  64.3 10.6 %collective-permute-start.9 = (bf16[2,384,128]{2,1,0:T(8,128)(2,1)}, bf16[2,384,128]{2,1,0:T(8,128)(2,1)S(1)}, u32[]{:S(2)}, u32[]{:S(2)}) collective-permute-start(bf16[2,384,128]{2,1,0:T(8,128)(2,1)} %get-tuple-element.32), channel_id=1, source_target_pairs={{0,12},{1,13},{2,14},{3,15},{4,0},{5,1},{6,2},{7,3},{8,4},{9,5},{1... | collective-permute-start | bytes 589832 | tf_op jit(solution)/shard_map/ppermute | solution.py:47
  65.0 10.0 %collective-permute-start.10 = (bf16[2,384,128]{2,1,0:T(8,128)(2,1)}, bf16[2,384,128]{2,1,0:T(8,128)(2,1)}, u32[]{:S(2)}, u32[]{:S(2)}) collective-permute-start(bf16[2,384,128]{2,1,0:T(8,128)(2,1)} %get-tuple-element.33), channel_id=1, source_target_pairs={{0,8},{1,9},{2,10},{3,11},{4,12},{5,13},{6,14},{7,15},{8,0},{9,1},... | collective-permute-start | bytes 589832 | tf_op jit(solution)/shard_map/ppermute | solution.py:47
  65.7 12.4 %collective-permute-start.11 = (bf16[2,384,128]{2,1,0:T(8,128)(2,1)}, bf16[2,384,128]{2,1,0:T(8,128)(2,1)}, u32[]{:S(2)}, u32[]{:S(2)}) collective-permute-start(bf16[2,384,128]{2,1,0:T(8,128)(2,1)} %get-tuple-element.34), channel_id=1, source_target_pairs={{0,4},{1,5},{2,6},{3,7},{4,8},{5,9},{6,10},{7,11},{8,12},{9,13},{1... | collective-permute-start | bytes 589832 | tf_op jit(solution)/shard_map/ppermute | solution.py:47
  79.4 7.0 %collective-permute-start.12 = (bf16[128,384]{1,0:T(8,128)(2,1)S(1)}, bf16[128,384]{1,0:T(8,128)(2,1)S(1)}, u32[]{:S(2)}, u32[]{:S(2)}) collective-permute-start(bf16[128,384]{1,0:T(8,128)(2,1)S(1)} %get-tuple-element.35.hop_ref), channel_id=1, source_target_pairs={{0,2},{1,3},{2,0},{3,1},{4,6},{5,7},{6,4},{7,5},{8,10},{9,11},{10,... | collective-permute-start | bytes 294920 | tf_op jit(solution)/shard_map/ppermute | solution.py:47
  81.3 7.4 %collective-permute-start.20 = (bf16[384,128]{1,0:T(8,128)(2,1)S(1)}, bf16[384,128]{1,0:T(8,128)(2,1)S(1)}, u32[]{:S(2)}, u32[]{:S(2)}) collective-permute-start(bf16[384,128]{1,0:T(8,128)(2,1)S(1)} %get-tuple-element.39), channel_id=1, source_target_pairs={{0,2},{1,3},{2,0},{3,1},{4,6},{5,7},{6,4},{7,5},{8,10},{9,11},{10,... | collective-permute-start | bytes 294920 | tf_op jit(solution)/shard_map/ppermute | solution.py:47
  86.4 18.7 %collective-permute-start.16 = (bf16[2,128,384]{2,1,0:T(8,128)(2,1)S(1)}, bf16[2,128,384]{2,1,0:T(8,128)(2,1)S(1)}, u32[]{:S(2)}, u32[]{:S(2)}) collective-permute-start(bf16[2,128,384]{2,1,0:T(8,128)(2,1)S(1)} %pad_maximum_fusion.2), channel_id=1, source_target_pairs={{0,1},{1,0},{2,3},{3,2},{4,5},{5,4},{6,7},{7,6},{8,9},{9,8},{10,11... | collective-permute-start | bytes 589832 | tf_op jit(solution)/shard_map/ppermute | solution.py:39
  86.5 9.4 %collective-permute-start.15 = (bf16[2,128,384]{2,1,0:T(8,128)(2,1)S(1)}, bf16[2,128,384]{2,1,0:T(8,128)(2,1)}, u32[]{:S(2)}, u32[]{:S(2)}) collective-permute-start(bf16[2,128,384]{2,1,0:T(8,128)(2,1)S(1)} %pad_maximum_fusion.2), channel_id=1, source_target_pairs={{0,12},{1,13},{2,14},{3,15},{4,0},{5,1},{6,2},{7,3},{8,4},{9,5},{1... | collective-permute-start | bytes 589832 | tf_op jit(solution)/shard_map/ppermute | solution.py:47
  87.3 9.4 %collective-permute-start.14 = (bf16[2,128,384]{2,1,0:T(8,128)(2,1)S(1)}, bf16[2,128,384]{2,1,0:T(8,128)(2,1)}, u32[]{:S(2)}, u32[]{:S(2)}) collective-permute-start(bf16[2,128,384]{2,1,0:T(8,128)(2,1)S(1)} %pad_maximum_fusion.2), channel_id=1, source_target_pairs={{0,8},{1,9},{2,10},{3,11},{4,12},{5,13},{6,14},{7,15},{8,0},{9,1},... | collective-permute-start | bytes 589832 | tf_op jit(solution)/shard_map/ppermute | solution.py:47
  88.1 12.0 %collective-permute-start.13 = (bf16[2,128,384]{2,1,0:T(8,128)(2,1)S(1)}, bf16[2,128,384]{2,1,0:T(8,128)(2,1)}, u32[]{:S(2)}, u32[]{:S(2)}) collective-permute-start(bf16[2,128,384]{2,1,0:T(8,128)(2,1)S(1)} %pad_maximum_fusion.2), channel_id=1, source_target_pairs={{0,4},{1,5},{2,6},{3,7},{4,8},{5,9},{6,10},{7,11},{8,12},{9,13},{1... | collective-permute-start | bytes 589832 | tf_op jit(solution)/shard_map/ppermute | solution.py:47
  89.6 18.6 %all-to-all-start.3 = ((bf16[8,384,128]{2,1,0:T(8,128)(2,1)}), bf16[8,384,128]{2,1,0:T(8,128)(2,1)}, u32[]{:S(2)}, u32[]{:S(2)}) async-start(bf16[8,384,128]{2,1,0:T(8,128)(2,1)} %shard_map.100), calls=%async_computation.3 | async-start | bytes 1572864 | tf_op jit(solution)/shard_map/all_to_all | solution.py:31
  95.9 9.2 %collective-permute-start.19 = (bf16[2,128,384]{2,1,0:T(8,128)(2,1)}, bf16[2,128,384]{2,1,0:T(8,128)(2,1)S(1)}, u32[]{:S(2)}, u32[]{:S(2)}) collective-permute-start(bf16[2,128,384]{2,1,0:T(8,128)(2,1)} %collective-permute-done.15), channel_id=1, source_target_pairs={{0,1},{1,0},{2,3},{3,2},{4,5},{5,4},{6,7},{7,6},{8,9},{9,8},{10,11... | collective-permute-start | bytes 589832 | tf_op jit(solution)/shard_map/ppermute | solution.py:39
  96.7 8.4 %collective-permute-start.18 = (bf16[2,128,384]{2,1,0:T(8,128)(2,1)}, bf16[2,128,384]{2,1,0:T(8,128)(2,1)S(1)}, u32[]{:S(2)}, u32[]{:S(2)}) collective-permute-start(bf16[2,128,384]{2,1,0:T(8,128)(2,1)} %collective-permute-done.14), channel_id=1, source_target_pairs={{0,1},{1,0},{2,3},{3,2},{4,5},{5,4},{6,7},{7,6},{8,9},{9,8},{10,11... | collective-permute-start | bytes 589832 | tf_op jit(solution)/shard_map/ppermute | solution.py:39
  100.1 5.0 %collective-permute-start.17 = (bf16[2,128,384]{2,1,0:T(8,128)(2,1)}, bf16[2,128,384]{2,1,0:T(8,128)(2,1)S(1)}, u32[]{:S(2)}, u32[]{:S(2)}) collective-permute-start(bf16[2,128,384]{2,1,0:T(8,128)(2,1)} %collective-permute-done.13), channel_id=1, source_target_pairs={{0,1},{1,0},{2,3},{3,2},{4,5},{5,4},{6,7},{7,6},{8,9},{9,8},{10,11... | collective-permute-start | bytes 589832 | tf_op jit(solution)/shard_map/ppermute | solution.py:39
  148.8 13.0 %all-to-all-start.5 = ((f32[8,64,128]{2,1,0:T(8,128)}), f32[8,64,128]{2,1,0:T(8,128)S(1)}, u32[]{:S(2)}, u32[]{:S(2)}) async-start(f32[8,64,128]{2,1,0:T(8,128)} %add.3), calls=%async_computation.5 | async-start | bytes 524288 | tf_op jit(solution)/shard_map/all_to_all | solution.py:35
  (14 other events, 102.5 us)
where the time goes:
time: 163 us; the launch traced here: 162 us
  waiting for transfers between devices  43.6 us (27%)
  Pallas kernels  37.1 us (23%)
  starting transfers between devices  35.6 us (22%)
  blocking collectives  32 us (20%)
  local copies, waits for them, and re-layouts  10.6 us (7%)
  other arithmetic  2.45 us (2%)
    pallas_call x10, Pallas kernels, call(): pl.pallas_call(kernel, grid=(steps,), in_specs=specs[:len(ins)], out_spec...  37.1 us
    all_to_all x2, blocking collectives, exchange_dst(): return lax.all_to_all(blocks, 'row', 0, 0)  32 us
    ppermute x12, waiting for transfers between devices, to_chip(): return lax.ppermute(blocks, 'col', pairs)  22.6 us
    ppermute x12, starting transfers between devices, to_chip(): return lax.ppermute(blocks, 'col', pairs)  16.5 us
    all_to_all x3, starting transfers between devices, exchange_dst(): return lax.all_to_all(blocks, 'row', 0, 0)  14.1 us
    all_to_all x3, waiting for transfers between devices, exchange_dst(): return lax.all_to_all(blocks, 'row', 0, 0)  10.5 us
    unnamed x35, local copies, waits for them, and re-layouts  8.91 us
    all_to_all x1, waiting for transfers between devices, exchange_src(): return lax.all_to_all(blocks, 'col', 0, 0, axis_index_groups=SAME_CORE)  7.76 us
  transfers between devices with their start and end apart: 26, of which 11 were waited for; matrix products, arithmetic and copies ran while one was open for 5% of the time, Pallas kernels for 4%

commit v1 on v0

--- a/solution.py
+++ b/solution.py
@@ -47,10 +47,9 @@
     return lax.ppermute(blocks, "col", pairs)
 
 
-def gather_src(block):
-    pair = jnp.stack([block, to_chip(block, 0, 1)])
+def gather_src(pair):
     pairs = [pair] + [to_chip(pair, dx, 0) for dx in range(1, 4)]
-    return jnp.concatenate(pairs), jnp.concatenate([swap_cores(p) for p in pairs])
+    return pairs, [swap_cores(p) for p in pairs]
 
 
 def array(*shape, dtype=BF16):
@@ -261,7 +260,9 @@
     mine_out[...] = total(0)
 
 
-def first_grad_kernel(mixed_ref, mine_ref, other_ref, out_ref):
+def first_grad_kernel(mixed_ref, mine_ref, other_ref, hop_ref, next_ref, out_ref, pair_ref):
+    pair_ref[0] = hop_ref[...]
+    pair_ref[1] = next_ref[...]
     grad = (mixed_ref[...] + (mine_ref[...] + other_ref[...].astype(F32))).astype(BF16)
     for block in range(GROUP):
         out_ref[block] = grad
@@ -276,10 +277,10 @@
 SECOND, ABOVE, BELOW, INNER, SHIFT, LAST = 0, 384, 448, 512, 536, 544
 
 
-def grad_kernel(
-    own_ref, other_ref, hop_own_ref, hop_other_ref, dst_ref, norm_ref, first_ref,
-    pack_ref, shift_ref, own_out, other_out, inner, mass, above, below, dst, grads, adj, wide, second,
-):
+def grad_kernel(own_ref, other_ref, *refs):
+    hop_own, hop_other, (dst_ref, norm_ref, first_ref) = refs[0:4], refs[4:8], refs[8:11]
+    pack_ref, shift_ref, own_out, other_out = refs[11:15]
+    inner, mass, above, below, dst, grads, adj, wide, second = refs[15:]
     step = pl.program_id(0)
     half = step % 2
 
@@ -295,7 +296,8 @@
     @pl.when(step < 2)
     def _():
         scores, weights = weights_of(src, dst[...], norm_ref)
-        hop = jnp.where(half == 0, hop_own_ref[...], hop_other_ref[...])
+        pieces = [jnp.where(half == 0, a[...], b[...]) for a, b in zip(hop_own, hop_other)]
+        hop = jnp.concatenate(pieces).reshape(GROUP * 128, 384)
         adj_grad = dot_nn(jnp.concatenate([hop, series_of(packed)], axis=1), grads[...])
         adj[half] = adj_grad
         wide[half] = jnp.where(scores > 0.0, weights, 0.0)
@@ -339,7 +341,7 @@
 
 
 def embed_grads(*ins):
-    rows = ins[4].shape[0] * 128
+    rows = GROUP * 128
     outs = [
         array(GROUP, LAST, 128),
         array(1, rows, dtype=F32),
@@ -423,7 +425,7 @@
 
 def local(dst_embed, src_embed, series, w_self, w_hop1, w_hop2, cotangent):
     src = call(source_kernel, 1, (src_embed.T, series), [array(160, 384)], vmem=60 * MIB)[0]
-    src_own, src_other = gather_src(src)
+    src_own, src_other = (jnp.concatenate(p) for p in gather_src(jnp.stack([src, to_chip(src, 0, 1)])))
     dst, first_mixed, base, mix1, mix2 = prepare(dst_embed.T, series, w_self, w_hop1, w_hop2, cotangent)
     dst = exchange_dst(dst)
     stats = exchange_dst(softmax_stats(src_own, src_other, dst))
@@ -436,11 +438,14 @@
         join_kernel, 1, (hop, *pairs), [array(128, 384), array(384, 128, dtype=F32), array(384, 128)]
     )
     rest = to_chip(rest, 0, 1)
-    first = call(first_grad_kernel, 1, (first_mixed, mine, rest), [array(GROUP, 384, 128)])[0]
+    first, hop_pair = call(
+        first_grad_kernel, 1, (first_mixed, mine, rest, hop, to_chip(hop, 0, 1)),
+        [array(GROUP, 384, 128), array(2, 128, 384)],
+    )
     first = exchange_dst(first)
-    hop_own, hop_other = (half.reshape(-1, 384) for half in gather_src(hop))
-
-    pack, shift, own, other = embed_grads(src_own, src_other, hop_own, hop_other, dst, norm, first)
+    hop_own, hop_other = gather_src(hop_pair)
+
+    pack, shift, own, other = embed_grads(src_own, src_other, *hop_own, *hop_other, dst, norm, first)
     pack = exchange_dst(pack)
     own, other = src_grads(src_own, src_other, dst, norm, pack, shift, own, other)
     output, d_dst = call(

time: 163 us -> 171 us (1.049)
  local copies, waits for them, and re-layouts: 10.6 us -> 16.7 us
  waiting for transfers between devices: 43.6 us -> 47.3 us
  Pallas kernels: 37.1 us -> 34.6 us
  blocking collectives: 32 us -> 34.3 us
    unnamed x35 -> x63, local copies, waits for them, and re-layouts: 8.91 us -> 16.7 us
    ppermute x12, waiting for transfers between devices: 22.6 us -> 27.9 us  [to_chip(): return lax.ppermute(blocks, 'col', pairs)]
    pallas_call x10, Pallas kernels: 37.1 us -> 34.6 us  [call(): pl.pallas_call(kernel, grid=(steps,), in_specs=specs[:len(ins)], out_spec...]
    all_to_all x2, blocking collectives: 32 us -> 34.3 us  [exchange_dst(): return lax.all_to_all(blocks, 'row', 0, 0)]
    all_to_all x3, waiting for transfers between devices: 10.5 us -> 8.71 us  [exchange_dst(): return lax.all_to_all(blocks, 'row', 0, 0)]
  transfers between devices with their start and end apart: 26 -> 26, of which waited for: 11 -> 12; matrix products, arithmetic and copies ran while one was open for 5% -> 0% of each run, Pallas kernels for 4% -> 4%
where the time goes in v1:
time: 171 us; the launch traced here: 170 us
  waiting for transfers between devices  47.3 us (28%)
  starting transfers between devices  35.1 us (21%)
  Pallas kernels  34.6 us (20%)
  blocking collectives  34.3 us (20%)
  local copies, waits for them, and re-layouts  16.7 us (10%)
    pallas_call x10, Pallas kernels, call(): pl.pallas_call(kernel, grid=(steps,), in_specs=specs[:len(ins)], out_spec...  34.6 us
    all_to_all x2, blocking collectives, exchange_dst(): return lax.all_to_all(blocks, 'row', 0, 0)  34.3 us
    ppermute x12, waiting for transfers between devices, to_chip(): return lax.ppermute(blocks, 'col', pairs)  27.9 us
    unnamed x63, local copies, waits for them, and re-layouts  16.7 us
    ppermute x12, starting transfers between devices, to_chip(): return lax.ppermute(blocks, 'col', pairs)  16.4 us
    all_to_all x3, starting transfers between devices, exchange_dst(): return lax.all_to_all(blocks, 'row', 0, 0)  13.9 us
    all_to_all x3, waiting for transfers between devices, exchange_dst(): return lax.all_to_all(blocks, 'row', 0, 0)  8.71 us
    all_to_all x1, waiting for transfers between devices, exchange_src(): return lax.all_to_all(blocks, 'col', 0, 0, axis_index_groups=SAME_CORE)  7.78 us
  transfers between devices with their start and end apart: 26, of which 12 were waited for; matrix products, arithmetic and copies ran while one was open for 0% of the time, Pallas kernels for 4%

profile of v1, /device:TPU:0, one launch (start us, length us, event | category | flops | bytes accessed | tf_op | source)
XLA Modules:
  0.0 170.4 jit_solution(15077105747490113072)
XLA Ops:
  0.6 1.6 shard_map.94
  2.2 4.0 %collective-permute-start = (bf16[160,384]{1,0:T(8,128)(2,1)}, bf16[160,384]{1,0:T(8,128)(2,1)S(1)}, u32[]{:S(2)}, u32[]{:S(2)}) collective-permute-start(bf16[160,384]{1,0:T(8,128)(2,1)} %shard_map.94), channel_id=1, source_target_pairs={{0,2},{1,3},{2,0},{3,1},{4,6},{5,7},{6,4},{7,5},{8,10},{9,11},{10,... | collective-permute-start | bytes 368648 | tf_op jit(solution)/shard_map/ppermute | solution.py:47
  6.2 3.2 %shard_map.95 = (bf16[8,448,128]{2,1,0:T(8,128)(2,1)}, f32[384,128]{1,0:T(8,128)}, f32[128,384]{1,0:T(8,128)}, bf16[384,384]{1,0:T(8,128)(2,1)}, bf16[384,384]{1,0:T(8,128)(2,1)}) custom-call(bf16[64,128]{1,0:T(8,128)(2,1)} %bitcast.13, bf16[128,384]{1,0:T(8,128)(2,1)} %series_ref.3, bf16[32,32]{1,0:T(8,128)(2,1)} %self_ref.1, bf16[32,32]{1,0:T(8,128)(2,1)} %hop1_ref.1, ...), custom_call_target="tpu_custom_call" | custom-call | flops 113246208 | bytes 2119680 | tf_op jit(solution)/shard_map/pallas_call | solution.py:71
  9.4 4.9 %all-to-all-start = ((bf16[8,448,128]{2,1,0:T(8,128)(2,1)}), bf16[8,448,128]{2,1,0:T(8,128)(2,1)S(1)}, u32[]{:S(2)}, u32[]{:S(2)}) async-start(bf16[8,448,128]{2,1,0:T(8,128)(2,1)} %get-tuple-element.30), calls=%async_computation | async-start | bytes 1835008 | tf_op jit(solution)/shard_map/all_to_all | solution.py:31
  14.5 2.8 %collective-permute-start.3 = (bf16[2,160,384]{2,1,0:T(8,128)(2,1)S(1)}, bf16[2,160,384]{2,1,0:T(8,128)(2,1)S(1)}, u32[]{:S(2)}, u32[]{:S(2)}) collective-permute-start(bf16[2,160,384]{2,1,0:T(8,128)(2,1)S(1)} %pad_maximum_fusion), channel_id=1, source_target_pairs={{0,12},{1,13},{2,14},{3,15},{4,0},{5,1},{6,2},{7,3},{8,4},{9,5},{1... | collective-permute-start | bytes 737288 | tf_op jit(solution)/shard_map/ppermute | solution.py:47
  19.0 9.4 %collective-permute-done.3 = bf16[2,160,384]{2,1,0:T(8,128)(2,1)S(1)} collective-permute-done((bf16[2,160,384]{2,1,0:T(8,128)(2,1)S(1)}, bf16[2,160,384]{2,1,0:T(8,128)(2,1)S(1)}, u32[]{:S(2)}, u32[]{:S(2)}) %collective-permute-start.3) | collective-permute-done | bytes 245792 | tf_op jit(solution)/shard_map/ppermute | solution.py:47
  28.9 3.2 %collective-permute-done.1 = bf16[2,160,384]{2,1,0:T(8,128)(2,1)S(1)} collective-permute-done((bf16[2,160,384]{2,1,0:T(8,128)(2,1)S(1)}, bf16[2,160,384]{2,1,0:T(8,128)(2,1)S(1)}, u32[]{:S(2)}, u32[]{:S(2)}) %collective-permute-start.1) | collective-permute-done | bytes 245792 | tf_op jit(solution)/shard_map/ppermute | solution.py:47
  33.8 3.0 %shard_map.96 = f32[8,2,1024]{2,1,0:T(2,128)S(1)} custom-call(bf16[8,160,384]{2,1,0:T(8,128)(2,1)S(1)} %constant_dynamic-update-slice_fusion.own_ref, bf16[8,160,384]{2,1,0:T(8,128)(2,1)S(1)} %constant_dynamic-update-slice_fusion.5.other_ref, bf16[8,448,128]{2,1,0:T(8,128)(2,1)S(1)} %all-to-all-done.dst_ref.refs_8_), custom_call_target="tpu_custom_call" | custom-call | flops 268435456 | bytes 2949120 | tf_op jit(solution)/shard_map/pallas_call | solution.py:71
  36.8 11.8 %all_to_all.30.stats_ref = f32[8,2,1024]{2,1,0:T(2,128)S(1)} all-to-all(f32[8,2,1024]{2,1,0:T(2,128)S(1)} %shard_map.96), channel_id=1, replica_groups=mesh['row'=8,'col'=16] {'row'}, dimensions={0} | all-to-all | bytes 131072 | tf_op jit(solution)/shard_map/all_to_all | solution.py:31
  48.7 7.1 %shard_map.97 = (f32[2,1024]{1,0:T(2,128)S(1)}, bf16[8,384,128]{2,1,0:T(8,128)(2,1)S(1)}, bf16[8,384,128]{2,1,0:T(8,128)(2,1)S(1)}, bf16[8,384,128]{2,1,0:T(8,128)(2,1)}) custom-call(bf16[8,160,384]{2,1,0:T(8,128)(2,1)S(1)} %constant_dynamic-update-slice_fusion.own_ref, bf16[8,160,384]{2,1,0:T(8,128)(2,1)S(1)} %constant_dynamic-update-slice_fusion.5.other_ref, ...), custom_call_target="tpu_custom_call" | custom-call | flops 3489660928 | bytes 5316608 | tf_op jit(solution)/shard_map/pallas_call | solution.py:71
  57.5 3.7 %all-to-all-start.2 = ((bf16[8,384,128]{2,1,0:T(8,128)(2,1)}), bf16[8,384,128]{2,1,0:T(8,128)(2,1)S(1)}, u32[]{:S(2)}, u32[]{:S(2)}) async-start(bf16[8,384,128]{2,1,0:T(8,128)(2,1)} %copy-done.4), calls=%async_computation.2 | async-start | bytes 1572864 | tf_op jit(solution)/shard_map/all_to_all | solution.py:31
  61.2 2.0 %shard_map.98 = (bf16[2,384,128]{2,1,0:T(8,128)(2,1)S(1)}, bf16[2,384,128]{2,1,0:T(8,128)(2,1)}, bf16[2,384,128]{2,1,0:T(8,128)(2,1)}, bf16[2,384,128]{2,1,0:T(8,128)(2,1)}) custom-call(bf16[8,384,128]{2,1,0:T(8,128)(2,1)S(1)} %copy-done.6, bf16[8,384,128]{2,1,0:T(8,128)(2,1)} %collective-permute-done.8.other_ref), custom_call_target="tpu_custom_call" | custom-call | bytes 2359296 | tf_op jit(solution)/shard_map/pallas_call | solution.py:71
  66.2 8.7 %all-to-all-done.2.hop_ref = bf16[8,384,128]{2,1,0:T(8,128)(2,1)S(1)} async-done(((bf16[8,384,128]{2,1,0:T(8,128)(2,1)}), bf16[8,384,128]{2,1,0:T(8,128)(2,1)S(1)}, u32[]{:S(2)}, u32[]{:S(2)}) %all-to-all-start.2) | async-done | bytes 786464 | tf_op jit(solution)/shard_map/all_to_all | solution.py:31
  74.9 2.6 %collective-permute-done.11.d_ref = bf16[2,384,128]{2,1,0:T(8,128)(2,1)S(1)} collective-permute-done((bf16[2,384,128]{2,1,0:T(8,128)(2,1)}, bf16[2,384,128]{2,1,0:T(8,128)(2,1)S(1)}, u32[]{:S(2)}, u32[]{:S(2)}) %collective-permute-start.11) | collective-permute-done | bytes 196640 | tf_op jit(solution)/shard_map/ppermute | solution.py:47
  79.8 2.4 %collective-permute-start.13 = (bf16[128,384]{1,0:T(8,128)(2,1)S(1)}, bf16[128,384]{1,0:T(8,128)(2,1)S(1)}, u32[]{:S(2)}, u32[]{:S(2)}) collective-permute-start(bf16[128,384]{1,0:T(8,128)(2,1)S(1)} %get-tuple-element.40.hop_ref), channel_id=1, source_target_pairs={{0,2},{1,3},{2,0},{3,1},{4,6},{5,7},{6,4},{7,5},{8,10},{9,11},{10,... | collective-permute-start | bytes 294920 | tf_op jit(solution)/shard_map/ppermute | solution.py:47
  82.2 3.6 %collective-permute-done.12.other_ref = bf16[384,128]{1,0:T(8,128)(2,1)S(1)} collective-permute-done((bf16[384,128]{1,0:T(8,128)(2,1)S(1)}, bf16[384,128]{1,0:T(8,128)(2,1)S(1)}, u32[]{:S(2)}, u32[]{:S(2)}) %collective-permute-start.12) | collective-permute-done | bytes 98336 | tf_op jit(solution)/shard_map/ppermute | solution.py:47
  88.9 5.3 %all-to-all-start.3 = ((bf16[8,384,128]{2,1,0:T(8,128)(2,1)}), bf16[8,384,128]{2,1,0:T(8,128)(2,1)}, u32[]{:S(2)}, u32[]{:S(2)}) async-start(bf16[8,384,128]{2,1,0:T(8,128)(2,1)} %copy-done.3), calls=%async_computation.3 | async-start | bytes 1572864 | tf_op jit(solution)/shard_map/all_to_all | solution.py:31
  96.4 5.7 %collective-permute-done.16.refs_3_ = bf16[2,128,384]{2,1,0:T(8,128)(2,1)S(1)} collective-permute-done((bf16[2,128,384]{2,1,0:T(8,128)(2,1)S(1)}, bf16[2,128,384]{2,1,0:T(8,128)(2,1)S(1)}, u32[]{:S(2)}, u32[]{:S(2)}) %collective-permute-start.16) | collective-permute-done | bytes 196640 | tf_op jit(solution)/shard_map/ppermute | solution.py:47
  115.7 12.8 %shard_map.101 = (bf16[8,544,128]{2,1,0:T(8,128)(2,1)S(1)}, f32[1,1024]{1,0:T(1,128)S(1)}, f32[8,64,128]{2,1,0:T(8,128)S(1)}, f32[8,64,128]{2,1,0:T(8,128)S(1)}) custom-call(bf16[8,160,384]{2,1,0:T(8,128)(2,1)S(1)} %copy-done.1, bf16[8,160,384]{2,1,0:T(8,128)(2,1)S(1)} %constant_dynamic-update-slice_fusion.5.other_ref, ...), custom_call_target="tpu_custom_call" | custom-call | flops 5905580032 | bytes 6893568 | tf_op jit(solution)/shard_map/pallas_call | solution.py:71
  128.5 22.5 %all_to_all.31.pack_ref = bf16[8,544,128]{2,1,0:T(8,128)(2,1)S(1)} all-to-all(bf16[8,544,128]{2,1,0:T(8,128)(2,1)S(1)} %get-tuple-element.44), channel_id=1, replica_groups=mesh['row'=8,'col'=16] {'row'}, dimensions={0} | all-to-all | bytes 2228224 | tf_op jit(solution)/shard_map/all_to_all | solution.py:31
  150.9 3.6 %shard_map.103 = (f32[8,64,128]{2,1,0:T(8,128)S(1)}, f32[8,64,128]{2,1,0:T(8,128)S(1)}) custom-call(bf16[8,160,384]{2,1,0:T(8,128)(2,1)S(1)} %copy-done.2, bf16[8,160,384]{2,1,0:T(8,128)(2,1)S(1)} %constant_dynamic-update-slice_fusion.5.other_ref, bf16[8,448,128]{2,1,0:T(8,128)(2,1)S(1)} %all-to-all-done.dst_ref.refs_8_, ...), custom_call_target="tpu_custom_call" | custom-call | flops 536870912 | bytes 5058560 | tf_op jit(solution)/shard_map/pallas_call | solution.py:71
  154.7 1.5 collective-permute-done.21
  157.0 4.0 %all-to-all-start.5 = ((f32[8,64,128]{2,1,0:T(8,128)}), f32[8,64,128]{2,1,0:T(8,128)S(1)}, u32[]{:S(2)}, u32[]{:S(2)}) async-start(f32[8,64,128]{2,1,0:T(8,128)} %add.3), calls=%async_computation.5 | async-start | bytes 524288 | tf_op jit(solution)/shard_map/all_to_all | solution.py:35
  162.0 7.8 %all-to-all-done.5 = f32[8,64,128]{2,1,0:T(8,128)S(1)} async-done(((f32[8,64,128]{2,1,0:T(8,128)}), f32[8,64,128]{2,1,0:T(8,128)S(1)}, u32[]{:S(2)}, u32[]{:S(2)}) %all-to-all-start.5) | async-done | bytes 262176 | tf_op jit(solution)/shard_map/all_to_all | solution.py:35
  (108 shorter events, 32.3 us)
Async XLA Ops:
  2.2 12.1 %collective-permute-start = (bf16[160,384]{1,0:T(8,128)(2,1)}, bf16[160,384]{1,0:T(8,128)(2,1)S(1)}, u32[]{:S(2)}, u32[]{:S(2)}) collective-permute-start(bf16[160,384]{1,0:T(8,128)(2,1)} %shard_map.94), channel_id=1, source_target_pairs={{0,2},{1,3},{2,0},{3,1},{4,6},{5,7},{6,4},{7,5},{8,10},{9,11},{10,... | collective-permute-start | bytes 368648 | tf_op jit(solution)/shard_map/ppermute | solution.py:47
  9.4 24.4 %all-to-all-start = ((bf16[8,448,128]{2,1,0:T(8,128)(2,1)}), bf16[8,448,128]{2,1,0:T(8,128)(2,1)S(1)}, u32[]{:S(2)}, u32[]{:S(2)}) async-start(bf16[8,448,128]{2,1,0:T(8,128)(2,1)} %get-tuple-element.30), calls=%async_computation | async-start | bytes 1835008 | tf_op jit(solution)/shard_map/all_to_all | solution.py:31
  14.4 17.7 %collective-permute-start.4 = (bf16[2,160,384]{2,1,0:T(8,128)(2,1)S(1)}, bf16[2,160,384]{2,1,0:T(8,128)(2,1)S(1)}, u32[]{:S(2)}, u32[]{:S(2)}) collective-permute-start(bf16[2,160,384]{2,1,0:T(8,128)(2,1)S(1)} %pad_maximum_fusion), channel_id=1, source_target_pairs={{0,1},{1,0},{2,3},{3,2},{4,5},{5,4},{6,7},{7,6},{8,9},{9,8},{10,11... | collective-permute-start | bytes 737288 | tf_op jit(solution)/shard_map/ppermute | solution.py:39
  14.5 13.9 %collective-permute-start.3 = (bf16[2,160,384]{2,1,0:T(8,128)(2,1)S(1)}, bf16[2,160,384]{2,1,0:T(8,128)(2,1)S(1)}, u32[]{:S(2)}, u32[]{:S(2)}) collective-permute-start(bf16[2,160,384]{2,1,0:T(8,128)(2,1)S(1)} %pad_maximum_fusion), channel_id=1, source_target_pairs={{0,12},{1,13},{2,14},{3,15},{4,0},{5,1},{6,2},{7,3},{8,4},{9,5},{1... | collective-permute-start | bytes 737288 | tf_op jit(solution)/shard_map/ppermute | solution.py:47
  17.3 11.1 %collective-permute-start.2 = (bf16[2,160,384]{2,1,0:T(8,128)(2,1)S(1)}, bf16[2,160,384]{2,1,0:T(8,128)(2,1)S(1)}, u32[]{:S(2)}, u32[]{:S(2)}) collective-permute-start(bf16[2,160,384]{2,1,0:T(8,128)(2,1)S(1)} %pad_maximum_fusion), channel_id=1, source_target_pairs={{0,8},{1,9},{2,10},{3,11},{4,12},{5,13},{6,14},{7,15},{8,0},{9,1},... | collective-permute-start | bytes 737288 | tf_op jit(solution)/shard_map/ppermute | solution.py:47
  18.1 14.0 %collective-permute-start.1 = (bf16[2,160,384]{2,1,0:T(8,128)(2,1)S(1)}, bf16[2,160,384]{2,1,0:T(8,128)(2,1)S(1)}, u32[]{:S(2)}, u32[]{:S(2)}) collective-permute-start(bf16[2,160,384]{2,1,0:T(8,128)(2,1)S(1)} %pad_maximum_fusion), channel_id=1, source_target_pairs={{0,4},{1,5},{2,6},{3,7},{4,8},{5,9},{6,10},{7,11},{8,12},{9,13},{1... | collective-permute-start | bytes 737288 | tf_op jit(solution)/shard_map/ppermute | solution.py:47
  28.4 5.3 %collective-permute-start.7 = (bf16[2,160,384]{2,1,0:T(8,128)(2,1)S(1)}, bf16[2,160,384]{2,1,0:T(8,128)(2,1)S(1)}, u32[]{:S(2)}, u32[]{:S(2)}) collective-permute-start(bf16[2,160,384]{2,1,0:T(8,128)(2,1)S(1)} %collective-permute-done.3), channel_id=1, source_target_pairs={{0,1},{1,0},{2,3},{3,2},{4,5},{5,4},{6,7},{7,6},{8,9},{9,8},{10,11... | collective-permute-start | bytes 737288 | tf_op jit(solution)/shard_map/ppermute | solution.py:39
  28.4 5.2 %collective-permute-start.6 = (bf16[2,160,384]{2,1,0:T(8,128)(2,1)S(1)}, bf16[2,160,384]{2,1,0:T(8,128)(2,1)S(1)}, u32[]{:S(2)}, u32[]{:S(2)}) collective-permute-start(bf16[2,160,384]{2,1,0:T(8,128)(2,1)S(1)} %collective-permute-done.2), channel_id=1, source_target_pairs={{0,1},{1,0},{2,3},{3,2},{4,5},{5,4},{6,7},{7,6},{8,9},{9,8},{10,11... | collective-permute-start | bytes 737288 | tf_op jit(solution)/shard_map/ppermute | solution.py:39
  57.5 3.7 %collective-permute-start.8 = (bf16[8,384,128]{2,1,0:T(8,128)(2,1)}, bf16[8,384,128]{2,1,0:T(8,128)(2,1)}, u32[]{:S(2)}, u32[]{:S(2)}) collective-permute-start(bf16[8,384,128]{2,1,0:T(8,128)(2,1)} %get-tuple-element.33), channel_id=1, source_target_pairs={{0,1},{1,0},{2,3},{3,2},{4,5},{5,4},{6,7},{7,6},{8,9},{9,8},{10,11... | collective-permute-start | bytes 2359304 | tf_op jit(solution)/shard_map/ppermute | solution.py:39
  57.5 17.3 %all-to-all-start.2 = ((bf16[8,384,128]{2,1,0:T(8,128)(2,1)}), bf16[8,384,128]{2,1,0:T(8,128)(2,1)S(1)}, u32[]{:S(2)}, u32[]{:S(2)}) async-start(bf16[8,384,128]{2,1,0:T(8,128)(2,1)} %copy-done.4), calls=%async_computation.2 | async-start | bytes 1572864 | tf_op jit(solution)/shard_map/all_to_all | solution.py:31
  63.9 10.9 %collective-permute-start.9 = (bf16[2,384,128]{2,1,0:T(8,128)(2,1)}, bf16[2,384,128]{2,1,0:T(8,128)(2,1)S(1)}, u32[]{:S(2)}, u32[]{:S(2)}) collective-permute-start(bf16[2,384,128]{2,1,0:T(8,128)(2,1)} %get-tuple-element.35), channel_id=1, source_target_pairs={{0,12},{1,13},{2,14},{3,15},{4,0},{5,1},{6,2},{7,3},{8,4},{9,5},{1... | collective-permute-start | bytes 589832 | tf_op jit(solution)/shard_map/ppermute | solution.py:47
  64.6 10.2 %collective-permute-start.10 = (bf16[2,384,128]{2,1,0:T(8,128)(2,1)}, bf16[2,384,128]{2,1,0:T(8,128)(2,1)S(1)}, u32[]{:S(2)}, u32[]{:S(2)}) collective-permute-start(bf16[2,384,128]{2,1,0:T(8,128)(2,1)} %get-tuple-element.36), channel_id=1, source_target_pairs={{0,8},{1,9},{2,10},{3,11},{4,12},{5,13},{6,14},{7,15},{8,0},{9,1},... | collective-permute-start | bytes 589832 | tf_op jit(solution)/shard_map/ppermute | solution.py:47
  65.3 12.1 %collective-permute-start.11 = (bf16[2,384,128]{2,1,0:T(8,128)(2,1)}, bf16[2,384,128]{2,1,0:T(8,128)(2,1)S(1)}, u32[]{:S(2)}, u32[]{:S(2)}) collective-permute-start(bf16[2,384,128]{2,1,0:T(8,128)(2,1)} %get-tuple-element.37), channel_id=1, source_target_pairs={{0,4},{1,5},{2,6},{3,7},{4,8},{5,9},{6,10},{7,11},{8,12},{9,13},{1... | collective-permute-start | bytes 589832 | tf_op jit(solution)/shard_map/ppermute | solution.py:47
  78.6 7.2 %collective-permute-start.12 = (bf16[384,128]{1,0:T(8,128)(2,1)S(1)}, bf16[384,128]{1,0:T(8,128)(2,1)S(1)}, u32[]{:S(2)}, u32[]{:S(2)}) collective-permute-start(bf16[384,128]{1,0:T(8,128)(2,1)S(1)} %get-tuple-element.39), channel_id=1, source_target_pairs={{0,2},{1,3},{2,0},{3,1},{4,6},{5,7},{6,4},{7,5},{8,10},{9,11},{10,... | collective-permute-start | bytes 294920 | tf_op jit(solution)/shard_map/ppermute | solution.py:47
  79.8 7.2 %collective-permute-start.13 = (bf16[128,384]{1,0:T(8,128)(2,1)S(1)}, bf16[128,384]{1,0:T(8,128)(2,1)S(1)}, u32[]{:S(2)}, u32[]{:S(2)}) collective-permute-start(bf16[128,384]{1,0:T(8,128)(2,1)S(1)} %get-tuple-element.40.hop_ref), channel_id=1, source_target_pairs={{0,2},{1,3},{2,0},{3,1},{4,6},{5,7},{6,4},{7,5},{8,10},{9,11},{10,... | collective-permute-start | bytes 294920 | tf_op jit(solution)/shard_map/ppermute | solution.py:47
  88.9 20.2 %all-to-all-start.3 = ((bf16[8,384,128]{2,1,0:T(8,128)(2,1)}), bf16[8,384,128]{2,1,0:T(8,128)(2,1)}, u32[]{:S(2)}, u32[]{:S(2)}) async-start(bf16[8,384,128]{2,1,0:T(8,128)(2,1)} %copy-done.3), calls=%async_computation.3 | async-start | bytes 1572864 | tf_op jit(solution)/shard_map/all_to_all | solution.py:31
  94.3 7.8 %collective-permute-start.16 = (bf16[2,128,384]{2,1,0:T(8,128)(2,1)S(1)}, bf16[2,128,384]{2,1,0:T(8,128)(2,1)S(1)}, u32[]{:S(2)}, u32[]{:S(2)}) collective-permute-start(bf16[2,128,384]{2,1,0:T(8,128)(2,1)S(1)} %get-tuple-element.41.refs_0_), channel_id=1, source_target_pairs={{0,12},{1,13},{2,14},{3,15},{4,0},{5,1},{6,2},{7,3},{8,4},{9,5},{1... | collective-permute-start | bytes 589832 | tf_op jit(solution)/shard_map/ppermute | solution.py:47
  94.3 9.4 %collective-permute-start.15 = (bf16[2,128,384]{2,1,0:T(8,128)(2,1)S(1)}, bf16[2,128,384]{2,1,0:T(8,128)(2,1)S(1)}, u32[]{:S(2)}, u32[]{:S(2)}) collective-permute-start(bf16[2,128,384]{2,1,0:T(8,128)(2,1)S(1)} %get-tuple-element.41.refs_0_), channel_id=1, source_target_pairs={{0,8},{1,9},{2,10},{3,11},{4,12},{5,13},{6,14},{7,15},{8,0},{9,1},... | collective-permute-start | bytes 589832 | tf_op jit(solution)/shard_map/ppermute | solution.py:47
  95.1 10.7 %collective-permute-start.14 = (bf16[2,128,384]{2,1,0:T(8,128)(2,1)S(1)}, bf16[2,128,384]{2,1,0:T(8,128)(2,1)S(1)}, u32[]{:S(2)}, u32[]{:S(2)}) collective-permute-start(bf16[2,128,384]{2,1,0:T(8,128)(2,1)S(1)} %get-tuple-element.41.refs_0_), channel_id=1, source_target_pairs={{0,4},{1,5},{2,6},{3,7},{4,8},{5,9},{6,10},{7,11},{8,12},{9,13},{1... | collective-permute-start | bytes 589832 | tf_op jit(solution)/shard_map/ppermute | solution.py:47
  96.4 10.0 %collective-permute-start.17 = (bf16[2,128,384]{2,1,0:T(8,128)(2,1)S(1)}, bf16[2,128,384]{2,1,0:T(8,128)(2,1)S(1)}, u32[]{:S(2)}, u32[]{:S(2)}) collective-permute-start(bf16[2,128,384]{2,1,0:T(8,128)(2,1)S(1)} %get-tuple-element.41.refs_0_), channel_id=1, source_target_pairs={{0,1},{1,0},{2,3},{3,2},{4,5},{5,4},{6,7},{7,6},{8,9},{9,8},{10,11... | collective-permute-start | bytes 589832 | tf_op jit(solution)/shard_map/ppermute | solution.py:39
  102.1 5.0 %collective-permute-start.20 = (bf16[2,128,384]{2,1,0:T(8,128)(2,1)S(1)}, bf16[2,128,384]{2,1,0:T(8,128)(2,1)S(1)}, u32[]{:S(2)}, u32[]{:S(2)}) collective-permute-start(bf16[2,128,384]{2,1,0:T(8,128)(2,1)S(1)} %collective-permute-done.16.refs_3_), channel_id=1, source_target_pairs={{0,1},{1,0},{2,3},{3,2},{4,5},{5,4},{6,7},{7,6},{8,9},{9,8},{10,11... | collective-permute-start | bytes 589832 | tf_op jit(solution)/shard_map/ppermute | solution.py:39
  103.7 4.1 %collective-permute-start.19 = (bf16[2,128,384]{2,1,0:T(8,128)(2,1)S(1)}, bf16[2,128,384]{2,1,0:T(8,128)(2,1)S(1)}, u32[]{:S(2)}, u32[]{:S(2)}) collective-permute-start(bf16[2,128,384]{2,1,0:T(8,128)(2,1)S(1)} %collective-permute-done.15.refs_2_), channel_id=1, source_target_pairs={{0,1},{1,0},{2,3},{3,2},{4,5},{5,4},{6,7},{7,6},{8,9},{9,8},{10,11... | collective-permute-start | bytes 589832 | tf_op jit(solution)/shard_map/ppermute | solution.py:39
  105.8 2.7 %collective-permute-start.18 = (bf16[2,128,384]{2,1,0:T(8,128)(2,1)S(1)}, bf16[2,128,384]{2,1,0:T(8,128)(2,1)S(1)}, u32[]{:S(2)}, u32[]{:S(2)}) collective-permute-start(bf16[2,128,384]{2,1,0:T(8,128)(2,1)S(1)} %collective-permute-done.14.refs_1_), channel_id=1, source_target_pairs={{0,1},{1,0},{2,3},{3,2},{4,5},{5,4},{6,7},{7,6},{8,9},{9,8},{10,11... | collective-permute-start | bytes 589832 | tf_op jit(solution)/shard_map/ppermute | solution.py:39
  157.0 12.8 %all-to-all-start.5 = ((f32[8,64,128]{2,1,0:T(8,128)}), f32[8,64,128]{2,1,0:T(8,128)S(1)}, u32[]{:S(2)}, u32[]{:S(2)}) async-start(f32[8,64,128]{2,1,0:T(8,128)} %add.3), calls=%async_computation.5 | async-start | bytes 524288 | tf_op jit(solution)/shard_map/all_to_all | solution.py:35
  (30 other events, 110.6 us)

commit v2 on v1

--- a/solution.py
+++ b/solution.py
@@ -277,10 +277,15 @@
 SECOND, ABOVE, BELOW, INNER, SHIFT, LAST = 0, 384, 448, 512, 536, 544
 
 
-def grad_kernel(own_ref, other_ref, *refs):
-    hop_own, hop_other, (dst_ref, norm_ref, first_ref) = refs[0:4], refs[4:8], refs[8:11]
-    pack_ref, shift_ref, own_out, other_out = refs[11:15]
-    inner, mass, above, below, dst, grads, adj, wide, second = refs[15:]
+def pieces_kernel(*refs):
+    for place, ref in enumerate(refs[:-1]):
+        refs[-1][256 * place : 256 * place + 256, :] = ref[...].reshape(256, 384)
+
+
+def grad_kernel(
+    own_ref, other_ref, hop_ref, dst_ref, norm_ref, first_ref,
+    pack_ref, shift_ref, own_out, other_out, inner, mass, above, below, dst, grads, adj, wide, second,
+):
     step = pl.program_id(0)
     half = step % 2
 
@@ -296,8 +301,7 @@
     @pl.when(step < 2)
     def _():
         scores, weights = weights_of(src, dst[...], norm_ref)
-        pieces = [jnp.where(half == 0, a[...], b[...]) for a, b in zip(hop_own, hop_other)]
-        hop = jnp.concatenate(pieces).reshape(GROUP * 128, 384)
+        hop = hop_ref[...]
         adj_grad = dot_nn(jnp.concatenate([hop, series_of(packed)], axis=1), grads[...])
         adj[half] = adj_grad
         wide[half] = jnp.where(scores > 0.0, weights, 0.0)
@@ -360,9 +364,13 @@
         pltpu.VMEM((384, rows), F32),
     ]
 
+
+    def first_pass(a):
+        return pl.BlockSpec((a.shape[0] // 2, a.shape[1]), lambda i: (jnp.minimum(i, 1), 0))
+
     size = 2 * rows * rows
     return call(
-        grad_kernel, 4, ins, outs, scratch, 2 * 1408 * size, size, vmem=46 * MIB
+        grad_kernel, 4, ins, outs, scratch, 2 * 1408 * size, size, kinds={2: first_pass}, vmem=46 * MIB
     )
 
 
@@ -444,8 +452,9 @@
     )
     first = exchange_dst(first)
     hop_own, hop_other = gather_src(hop_pair)
-
-    pack, shift, own, other = embed_grads(src_own, src_other, *hop_own, *hop_other, dst, norm, first)
+    hop_all = call(pieces_kernel, 1, (*hop_own, *hop_other), [array(2 * GROUP * 128, 384)])[0]
+
+    pack, shift, own, other = embed_grads(src_own, src_other, hop_all, dst, norm, first)
     pack = exchange_dst(pack)
     own, other = src_grads(src_own, src_other, dst, norm, pack, shift, own, other)
     output, d_dst = call(

time: 171 us -> 164 us (0.959)
  local copies, waits for them, and re-layouts: 16.7 us -> 7.25 us
  waiting for transfers between devices: 47.3 us -> 50.1 us
    unnamed x63 -> x37, local copies, waits for them, and re-layouts: 16.7 us -> 7.16 us
    pallas_call x10 -> x11, Pallas kernels: 34.6 us -> 35.5 us  [call(): pl.pallas_call(kernel, grid=(steps,), in_specs=specs[:len(ins)], out_spec...]
  transfers between devices with their start and end apart: 26 -> 26, of which waited for: 12 -> 13; matrix products, arithmetic and copies ran while one was open for 0% -> 0% of each run, Pallas kernels for 4% -> 4%
where the time goes in v2:
time: 164 us
  waiting for transfers between devices  50.1 us (31%)
  Pallas kernels  35.5 us (22%)
  starting transfers between devices  34.7 us (21%)
  blocking collectives  33.9 us (21%)
  local copies, waits for them, and re-layouts  7.25 us (4%)
    pallas_call x11, Pallas kernels, call(): pl.pallas_call(kernel, grid=(steps,), in_specs=specs[:len(ins)], out_spec...  35.5 us
    all_to_all x2, blocking collectives, exchange_dst(): return lax.all_to_all(blocks, 'row', 0, 0)  33.9 us
    ppermute x12, waiting for transfers between devices, to_chip(): return lax.ppermute(blocks, 'col', pairs)  29.3 us
    ppermute x12, starting transfers between devices, to_chip(): return lax.ppermute(blocks, 'col', pairs)  16.5 us
    all_to_all x3, starting transfers between devices, exchange_dst(): return lax.all_to_all(blocks, 'row', 0, 0)  13.9 us
    all_to_all x3, waiting for transfers between devices, exchange_dst(): return lax.all_to_all(blocks, 'row', 0, 0)  8.71 us
    all_to_all x1, waiting for transfers between devices, exchange_src(): return lax.all_to_all(blocks, 'col', 0, 0, axis_index_groups=SAME_CORE)  7.83 us
    unnamed x37, local copies, waits for them, and re-layouts  7.16 us
  transfers between devices with their start and end apart: 26, of which 13 were waited for; matrix products, arithmetic and copies ran while one was open for 0% of the time, Pallas kernels for 4%

profile of v2, /device:TPU:0, one launch (start us, length us, event | category | flops | bytes accessed | tf_op | source)
XLA Modules:
  0.0 163.8 jit_solution(16300748826982591201)
XLA Ops:
  2.2 4.0 %collective-permute-start = (bf16[160,384]{1,0:T(8,128)(2,1)}, bf16[160,384]{1,0:T(8,128)(2,1)S(1)}, u32[]{:S(2)}, u32[]{:S(2)}) collective-permute-start(bf16[160,384]{1,0:T(8,128)(2,1)} %shard_map.94), channel_id=1, source_target_pairs={{0,2},{1,3},{2,0},{3,1},{4,6},{5,7},{6,4},{7,5},{8,10},{9,11},{10,... | collective-permute-start | bytes 368648 | tf_op jit(solution)/shard_map/ppermute | solution.py:47
  6.2 3.2 %shard_map.95 = (bf16[8,448,128]{2,1,0:T(8,128)(2,1)}, f32[384,128]{1,0:T(8,128)}, f32[128,384]{1,0:T(8,128)}, bf16[384,384]{1,0:T(8,128)(2,1)}, bf16[384,384]{1,0:T(8,128)(2,1)}) custom-call(bf16[64,128]{1,0:T(8,128)(2,1)} %bitcast.13, bf16[128,384]{1,0:T(8,128)(2,1)} %series_ref.3, bf16[32,32]{1,0:T(8,128)(2,1)} %self_ref.1, bf16[32,32]{1,0:T(8,128)(2,1)} %hop1_ref.1, ...), custom_call_target="tpu_custom_call" | custom-call | flops 113246208 | bytes 2119680 | tf_op jit(solution)/shard_map/pallas_call | solution.py:71
  9.4 4.9 %all-to-all-start = ((bf16[8,448,128]{2,1,0:T(8,128)(2,1)}), bf16[8,448,128]{2,1,0:T(8,128)(2,1)S(1)}, u32[]{:S(2)}, u32[]{:S(2)}) async-start(bf16[8,448,128]{2,1,0:T(8,128)(2,1)} %get-tuple-element.30), calls=%async_computation | async-start | bytes 1835008 | tf_op jit(solution)/shard_map/all_to_all | solution.py:31
  14.5 2.8 %collective-permute-start.3 = (bf16[2,160,384]{2,1,0:T(8,128)(2,1)S(1)}, bf16[2,160,384]{2,1,0:T(8,128)(2,1)S(1)}, u32[]{:S(2)}, u32[]{:S(2)}) collective-permute-start(bf16[2,160,384]{2,1,0:T(8,128)(2,1)S(1)} %pad_maximum_fusion), channel_id=1, source_target_pairs={{0,12},{1,13},{2,14},{3,15},{4,0},{5,1},{6,2},{7,3},{8,4},{9,5},{1... | collective-permute-start | bytes 737288 | tf_op jit(solution)/shard_map/ppermute | solution.py:47
  19.0 9.4 %collective-permute-done.3 = bf16[2,160,384]{2,1,0:T(8,128)(2,1)S(1)} collective-permute-done((bf16[2,160,384]{2,1,0:T(8,128)(2,1)S(1)}, bf16[2,160,384]{2,1,0:T(8,128)(2,1)S(1)}, u32[]{:S(2)}, u32[]{:S(2)}) %collective-permute-start.3) | collective-permute-done | bytes 245792 | tf_op jit(solution)/shard_map/ppermute | solution.py:47
  28.9 3.2 %collective-permute-done.1 = bf16[2,160,384]{2,1,0:T(8,128)(2,1)S(1)} collective-permute-done((bf16[2,160,384]{2,1,0:T(8,128)(2,1)S(1)}, bf16[2,160,384]{2,1,0:T(8,128)(2,1)S(1)}, u32[]{:S(2)}, u32[]{:S(2)}) %collective-permute-start.1) | collective-permute-done | bytes 245792 | tf_op jit(solution)/shard_map/ppermute | solution.py:47
  33.8 3.0 %shard_map.96 = f32[8,2,1024]{2,1,0:T(2,128)S(1)} custom-call(bf16[8,160,384]{2,1,0:T(8,128)(2,1)S(1)} %constant_dynamic-update-slice_fusion.own_ref, bf16[8,160,384]{2,1,0:T(8,128)(2,1)S(1)} %constant_dynamic-update-slice_fusion.5.other_ref, bf16[8,448,128]{2,1,0:T(8,128)(2,1)S(1)} %all-to-all-done.dst_ref), custom_call_target="tpu_custom_call" | custom-call | flops 268435456 | bytes 2949120 | tf_op jit(solution)/shard_map/pallas_call | solution.py:71
  36.8 11.8 %all_to_all.30.stats_ref = f32[8,2,1024]{2,1,0:T(2,128)S(1)} all-to-all(f32[8,2,1024]{2,1,0:T(2,128)S(1)} %shard_map.96), channel_id=1, replica_groups=mesh['row'=8,'col'=16] {'row'}, dimensions={0} | all-to-all | bytes 131072 | tf_op jit(solution)/shard_map/all_to_all | solution.py:31
  48.6 7.1 %shard_map.97 = (f32[2,1024]{1,0:T(2,128)S(1)}, bf16[8,384,128]{2,1,0:T(8,128)(2,1)S(1)}, bf16[8,384,128]{2,1,0:T(8,128)(2,1)S(1)}, bf16[8,384,128]{2,1,0:T(8,128)(2,1)}) custom-call(bf16[8,160,384]{2,1,0:T(8,128)(2,1)S(1)} %constant_dynamic-update-slice_fusion.own_ref, bf16[8,160,384]{2,1,0:T(8,128)(2,1)S(1)} %constant_dynamic-update-slice_fusion.5.other_ref, ...), custom_call_target="tpu_custom_call" | custom-call | flops 3489660928 | bytes 5316608 | tf_op jit(solution)/shard_map/pallas_call | solution.py:71
  57.5 3.7 %all-to-all-start.2 = ((bf16[8,384,128]{2,1,0:T(8,128)(2,1)}), bf16[8,384,128]{2,1,0:T(8,128)(2,1)S(1)}, u32[]{:S(2)}, u32[]{:S(2)}) async-start(bf16[8,384,128]{2,1,0:T(8,128)(2,1)} %copy-done.5), calls=%async_computation.2 | async-start | bytes 1572864 | tf_op jit(solution)/shard_map/all_to_all | solution.py:31
  61.2 2.0 %shard_map.98 = (bf16[2,384,128]{2,1,0:T(8,128)(2,1)S(1)}, bf16[2,384,128]{2,1,0:T(8,128)(2,1)}, bf16[2,384,128]{2,1,0:T(8,128)(2,1)}, bf16[2,384,128]{2,1,0:T(8,128)(2,1)}) custom-call(bf16[8,384,128]{2,1,0:T(8,128)(2,1)S(1)} %copy-done.7, bf16[8,384,128]{2,1,0:T(8,128)(2,1)} %collective-permute-done.8.other_ref), custom_call_target="tpu_custom_call" | custom-call | bytes 2359296 | tf_op jit(solution)/shard_map/pallas_call | solution.py:71
  66.1 8.7 %all-to-all-done.2.hop_ref = bf16[8,384,128]{2,1,0:T(8,128)(2,1)S(1)} async-done(((bf16[8,384,128]{2,1,0:T(8,128)(2,1)}), bf16[8,384,128]{2,1,0:T(8,128)(2,1)S(1)}, u32[]{:S(2)}, u32[]{:S(2)}) %all-to-all-start.2) | async-done | bytes 786464 | tf_op jit(solution)/shard_map/all_to_all | solution.py:31
  74.8 2.6 %collective-permute-done.11.d_ref = bf16[2,384,128]{2,1,0:T(8,128)(2,1)S(1)} collective-permute-done((bf16[2,384,128]{2,1,0:T(8,128)(2,1)}, bf16[2,384,128]{2,1,0:T(8,128)(2,1)S(1)}, u32[]{:S(2)}, u32[]{:S(2)}) %collective-permute-start.11) | collective-permute-done | bytes 196640 | tf_op jit(solution)/shard_map/ppermute | solution.py:47
  79.8 2.4 %collective-permute-start.13 = (bf16[128,384]{1,0:T(8,128)(2,1)S(1)}, bf16[128,384]{1,0:T(8,128)(2,1)S(1)}, u32[]{:S(2)}, u32[]{:S(2)}) collective-permute-start(bf16[128,384]{1,0:T(8,128)(2,1)S(1)} %get-tuple-element.40.hop_ref), channel_id=1, source_target_pairs={{0,2},{1,3},{2,0},{3,1},{4,6},{5,7},{6,4},{7,5},{8,10},{9,11},{10,... | collective-permute-start | bytes 294920 | tf_op jit(solution)/shard_map/ppermute | solution.py:47
  82.2 3.6 %collective-permute-done.12.other_ref = bf16[384,128]{1,0:T(8,128)(2,1)S(1)} collective-permute-done((bf16[384,128]{1,0:T(8,128)(2,1)S(1)}, bf16[384,128]{1,0:T(8,128)(2,1)S(1)}, u32[]{:S(2)}, u32[]{:S(2)}) %collective-permute-start.12) | collective-permute-done | bytes 98336 | tf_op jit(solution)/shard_map/ppermute | solution.py:47
  88.9 5.3 %all-to-all-start.3 = ((bf16[8,384,128]{2,1,0:T(8,128)(2,1)}), bf16[8,384,128]{2,1,0:T(8,128)(2,1)}, u32[]{:S(2)}, u32[]{:S(2)}) async-start(bf16[8,384,128]{2,1,0:T(8,128)(2,1)} %get-tuple-element.43), calls=%async_computation.3 | async-start | bytes 1572864 | tf_op jit(solution)/shard_map/all_to_all | solution.py:31
  96.4 5.6 %collective-permute-done.16.refs_3_ = bf16[2,128,384]{2,1,0:T(8,128)(2,1)S(1)} collective-permute-done((bf16[2,128,384]{2,1,0:T(8,128)(2,1)S(1)}, bf16[2,128,384]{2,1,0:T(8,128)(2,1)S(1)}, u32[]{:S(2)}, u32[]{:S(2)}) %collective-permute-start.16) | collective-permute-done | bytes 196640 | tf_op jit(solution)/shard_map/ppermute | solution.py:47
  102.1 1.6 collective-permute-done.15.refs_2_
  103.7 2.1 %collective-permute-done.14.refs_1_ = bf16[2,128,384]{2,1,0:T(8,128)(2,1)S(1)} collective-permute-done((bf16[2,128,384]{2,1,0:T(8,128)(2,1)S(1)}, bf16[2,128,384]{2,1,0:T(8,128)(2,1)S(1)}, u32[]{:S(2)}, u32[]{:S(2)}) %collective-permute-start.14) | collective-permute-done | bytes 196640 | tf_op jit(solution)/shard_map/ppermute | solution.py:47
  110.0 12.7 %shard_map.102 = (bf16[8,544,128]{2,1,0:T(8,128)(2,1)S(1)}, f32[1,1024]{1,0:T(1,128)S(1)}, f32[8,64,128]{2,1,0:T(8,128)S(1)}, f32[8,64,128]{2,1,0:T(8,128)S(1)}) custom-call(bf16[8,160,384]{2,1,0:T(8,128)(2,1)S(1)} %copy-done.3, bf16[8,160,384]{2,1,0:T(8,128)(2,1)S(1)} %constant_dynamic-update-slice_fusion.5.other_ref, bf16[2048,384]{1,0:T(8,128)(2,1)S(1)} %copy-done.1, ...), custom_call_target="tpu_custom_call" | custom-call | flops 5905580032 | bytes 6893568 | tf_op jit(solution)/shard_map/pallas_call | solution.py:71
  122.7 22.1 %all_to_all.31.pack_ref = bf16[8,544,128]{2,1,0:T(8,128)(2,1)S(1)} all-to-all(bf16[8,544,128]{2,1,0:T(8,128)(2,1)S(1)} %get-tuple-element.44), channel_id=1, replica_groups=mesh['row'=8,'col'=16] {'row'}, dimensions={0} | all-to-all | bytes 2228224 | tf_op jit(solution)/shard_map/all_to_all | solution.py:31
  144.8 3.6 %shard_map.104 = (f32[8,64,128]{2,1,0:T(8,128)S(1)}, f32[8,64,128]{2,1,0:T(8,128)S(1)}) custom-call(bf16[8,160,384]{2,1,0:T(8,128)(2,1)S(1)} %copy-done.4, bf16[8,160,384]{2,1,0:T(8,128)(2,1)S(1)} %constant_dynamic-update-slice_fusion.5.other_ref, bf16[8,448,128]{2,1,0:T(8,128)(2,1)S(1)} %all-to-all-done.dst_ref, f32[2,1024]{1,0:T(2,128)S(1)} %get-tuple-element.42.norm_ref, ...), custom_call_target="tpu_custom_call" | custom-call | flops 536870912 | bytes 5058560 | tf_op jit(solution)/shard_map/pallas_call | solution.py:71
  150.8 3.5 %all-to-all-start.5 = ((f32[8,64,128]{2,1,0:T(8,128)}), f32[8,64,128]{2,1,0:T(8,128)S(1)}, u32[]{:S(2)}, u32[]{:S(2)}) async-start(f32[8,64,128]{2,1,0:T(8,128)} %add.3), calls=%async_computation.5 | async-start | bytes 524288 | tf_op jit(solution)/shard_map/all_to_all | solution.py:35
  155.3 7.8 %all-to-all-done.5 = f32[8,64,128]{2,1,0:T(8,128)S(1)} async-done(((f32[8,64,128]{2,1,0:T(8,128)}), f32[8,64,128]{2,1,0:T(8,128)S(1)}, u32[]{:S(2)}, u32[]{:S(2)}) %all-to-all-start.5) | async-done | bytes 262176 | tf_op jit(solution)/shard_map/all_to_all | solution.py:35
  (83 shorter events, 26.1 us)
Async XLA Ops:
  2.2 12.1 %collective-permute-start = (bf16[160,384]{1,0:T(8,128)(2,1)}, bf16[160,384]{1,0:T(8,128)(2,1)S(1)}, u32[]{:S(2)}, u32[]{:S(2)}) collective-permute-start(bf16[160,384]{1,0:T(8,128)(2,1)} %shard_map.94), channel_id=1, source_target_pairs={{0,2},{1,3},{2,0},{3,1},{4,6},{5,7},{6,4},{7,5},{8,10},{9,11},{10,... | collective-permute-start | bytes 368648 | tf_op jit(solution)/shard_map/ppermute | solution.py:47
  9.4 24.4 %all-to-all-start = ((bf16[8,448,128]{2,1,0:T(8,128)(2,1)}), bf16[8,448,128]{2,1,0:T(8,128)(2,1)S(1)}, u32[]{:S(2)}, u32[]{:S(2)}) async-start(bf16[8,448,128]{2,1,0:T(8,128)(2,1)} %get-tuple-element.30), calls=%async_computation | async-start | bytes 1835008 | tf_op jit(solution)/shard_map/all_to_all | solution.py:31
  14.4 17.7 %collective-permute-start.4 = (bf16[2,160,384]{2,1,0:T(8,128)(2,1)S(1)}, bf16[2,160,384]{2,1,0:T(8,128)(2,1)S(1)}, u32[]{:S(2)}, u32[]{:S(2)}) collective-permute-start(bf16[2,160,384]{2,1,0:T(8,128)(2,1)S(1)} %pad_maximum_fusion), channel_id=1, source_target_pairs={{0,1},{1,0},{2,3},{3,2},{4,5},{5,4},{6,7},{7,6},{8,9},{9,8},{10,11... | collective-permute-start | bytes 737288 | tf_op jit(solution)/shard_map/ppermute | solution.py:39
  14.5 13.9 %collective-permute-start.3 = (bf16[2,160,384]{2,1,0:T(8,128)(2,1)S(1)}, bf16[2,160,384]{2,1,0:T(8,128)(2,1)S(1)}, u32[]{:S(2)}, u32[]{:S(2)}) collective-permute-start(bf16[2,160,384]{2,1,0:T(8,128)(2,1)S(1)} %pad_maximum_fusion), channel_id=1, source_target_pairs={{0,12},{1,13},{2,14},{3,15},{4,0},{5,1},{6,2},{7,3},{8,4},{9,5},{1... | collective-permute-start | bytes 737288 | tf_op jit(solution)/shard_map/ppermute | solution.py:47
  17.3 11.1 %collective-permute-start.2 = (bf16[2,160,384]{2,1,0:T(8,128)(2,1)S(1)}, bf16[2,160,384]{2,1,0:T(8,128)(2,1)S(1)}, u32[]{:S(2)}, u32[]{:S(2)}) collective-permute-start(bf16[2,160,384]{2,1,0:T(8,128)(2,1)S(1)} %pad_maximum_fusion), channel_id=1, source_target_pairs={{0,8},{1,9},{2,10},{3,11},{4,12},{5,13},{6,14},{7,15},{8,0},{9,1},... | collective-permute-start | bytes 737288 | tf_op jit(solution)/shard_map/ppermute | solution.py:47
  18.1 14.0 %collective-permute-start.1 = (bf16[2,160,384]{2,1,0:T(8,128)(2,1)S(1)}, bf16[2,160,384]{2,1,0:T(8,128)(2,1)S(1)}, u32[]{:S(2)}, u32[]{:S(2)}) collective-permute-start(bf16[2,160,384]{2,1,0:T(8,128)(2,1)S(1)} %pad_maximum_fusion), channel_id=1, source_target_pairs={{0,4},{1,5},{2,6},{3,7},{4,8},{5,9},{6,10},{7,11},{8,12},{9,13},{1... | collective-permute-start | bytes 737288 | tf_op jit(solution)/shard_map/ppermute | solution.py:47
  28.4 5.3 %collective-permute-start.7 = (bf16[2,160,384]{2,1,0:T(8,128)(2,1)S(1)}, bf16[2,160,384]{2,1,0:T(8,128)(2,1)S(1)}, u32[]{:S(2)}, u32[]{:S(2)}) collective-permute-start(bf16[2,160,384]{2,1,0:T(8,128)(2,1)S(1)} %collective-permute-done.3), channel_id=1, source_target_pairs={{0,1},{1,0},{2,3},{3,2},{4,5},{5,4},{6,7},{7,6},{8,9},{9,8},{10,11... | collective-permute-start | bytes 737288 | tf_op jit(solution)/shard_map/ppermute | solution.py:39
  28.4 5.2 %collective-permute-start.6 = (bf16[2,160,384]{2,1,0:T(8,128)(2,1)S(1)}, bf16[2,160,384]{2,1,0:T(8,128)(2,1)S(1)}, u32[]{:S(2)}, u32[]{:S(2)}) collective-permute-start(bf16[2,160,384]{2,1,0:T(8,128)(2,1)S(1)} %collective-permute-done.2), channel_id=1, source_target_pairs={{0,1},{1,0},{2,3},{3,2},{4,5},{5,4},{6,7},{7,6},{8,9},{9,8},{10,11... | collective-permute-start | bytes 737288 | tf_op jit(solution)/shard_map/ppermute | solution.py:39
  57.5 3.7 %collective-permute-start.8 = (bf16[8,384,128]{2,1,0:T(8,128)(2,1)}, bf16[8,384,128]{2,1,0:T(8,128)(2,1)}, u32[]{:S(2)}, u32[]{:S(2)}) collective-permute-start(bf16[8,384,128]{2,1,0:T(8,128)(2,1)} %get-tuple-element.33), channel_id=1, source_target_pairs={{0,1},{1,0},{2,3},{3,2},{4,5},{5,4},{6,7},{7,6},{8,9},{9,8},{10,11... | collective-permute-start | bytes 2359304 | tf_op jit(solution)/shard_map/ppermute | solution.py:39
  57.5 17.3 %all-to-all-start.2 = ((bf16[8,384,128]{2,1,0:T(8,128)(2,1)}), bf16[8,384,128]{2,1,0:T(8,128)(2,1)S(1)}, u32[]{:S(2)}, u32[]{:S(2)}) async-start(bf16[8,384,128]{2,1,0:T(8,128)(2,1)} %copy-done.5), calls=%async_computation.2 | async-start | bytes 1572864 | tf_op jit(solution)/shard_map/all_to_all | solution.py:31
  63.9 10.9 %collective-permute-start.9 = (bf16[2,384,128]{2,1,0:T(8,128)(2,1)}, bf16[2,384,128]{2,1,0:T(8,128)(2,1)S(1)}, u32[]{:S(2)}, u32[]{:S(2)}) collective-permute-start(bf16[2,384,128]{2,1,0:T(8,128)(2,1)} %get-tuple-element.35), channel_id=1, source_target_pairs={{0,12},{1,13},{2,14},{3,15},{4,0},{5,1},{6,2},{7,3},{8,4},{9,5},{1... | collective-permute-start | bytes 589832 | tf_op jit(solution)/shard_map/ppermute | solution.py:47
  64.6 10.3 %collective-permute-start.10 = (bf16[2,384,128]{2,1,0:T(8,128)(2,1)}, bf16[2,384,128]{2,1,0:T(8,128)(2,1)S(1)}, u32[]{:S(2)}, u32[]{:S(2)}) collective-permute-start(bf16[2,384,128]{2,1,0:T(8,128)(2,1)} %get-tuple-element.36), channel_id=1, source_target_pairs={{0,8},{1,9},{2,10},{3,11},{4,12},{5,13},{6,14},{7,15},{8,0},{9,1},... | collective-permute-start | bytes 589832 | tf_op jit(solution)/shard_map/ppermute | solution.py:47
  65.3 12.1 %collective-permute-start.11 = (bf16[2,384,128]{2,1,0:T(8,128)(2,1)}, bf16[2,384,128]{2,1,0:T(8,128)(2,1)S(1)}, u32[]{:S(2)}, u32[]{:S(2)}) collective-permute-start(bf16[2,384,128]{2,1,0:T(8,128)(2,1)} %get-tuple-element.37), channel_id=1, source_target_pairs={{0,4},{1,5},{2,6},{3,7},{4,8},{5,9},{6,10},{7,11},{8,12},{9,13},{1... | collective-permute-start | bytes 589832 | tf_op jit(solution)/shard_map/ppermute | solution.py:47
  78.6 7.2 %collective-permute-start.12 = (bf16[384,128]{1,0:T(8,128)(2,1)S(1)}, bf16[384,128]{1,0:T(8,128)(2,1)S(1)}, u32[]{:S(2)}, u32[]{:S(2)}) collective-permute-start(bf16[384,128]{1,0:T(8,128)(2,1)S(1)} %get-tuple-element.39), channel_id=1, source_target_pairs={{0,2},{1,3},{2,0},{3,1},{4,6},{5,7},{6,4},{7,5},{8,10},{9,11},{10,... | collective-permute-start | bytes 294920 | tf_op jit(solution)/shard_map/ppermute | solution.py:47
  79.8 7.2 %collective-permute-start.13 = (bf16[128,384]{1,0:T(8,128)(2,1)S(1)}, bf16[128,384]{1,0:T(8,128)(2,1)S(1)}, u32[]{:S(2)}, u32[]{:S(2)}) collective-permute-start(bf16[128,384]{1,0:T(8,128)(2,1)S(1)} %get-tuple-element.40.hop_ref), channel_id=1, source_target_pairs={{0,2},{1,3},{2,0},{3,1},{4,6},{5,7},{6,4},{7,5},{8,10},{9,11},{10,... | collective-permute-start | bytes 294920 | tf_op jit(solution)/shard_map/ppermute | solution.py:47
  88.9 19.7 %all-to-all-start.3 = ((bf16[8,384,128]{2,1,0:T(8,128)(2,1)}), bf16[8,384,128]{2,1,0:T(8,128)(2,1)}, u32[]{:S(2)}, u32[]{:S(2)}) async-start(bf16[8,384,128]{2,1,0:T(8,128)(2,1)} %get-tuple-element.43), calls=%async_computation.3 | async-start | bytes 1572864 | tf_op jit(solution)/shard_map/all_to_all | solution.py:31
  94.2 7.9 %collective-permute-start.16 = (bf16[2,128,384]{2,1,0:T(8,128)(2,1)S(1)}, bf16[2,128,384]{2,1,0:T(8,128)(2,1)S(1)}, u32[]{:S(2)}, u32[]{:S(2)}) collective-permute-start(bf16[2,128,384]{2,1,0:T(8,128)(2,1)S(1)} %get-tuple-element.41.refs_0_), channel_id=1, source_target_pairs={{0,12},{1,13},{2,14},{3,15},{4,0},{5,1},{6,2},{7,3},{8,4},{9,5},{1... | collective-permute-start | bytes 589832 | tf_op jit(solution)/shard_map/ppermute | solution.py:47
  94.3 9.4 %collective-permute-start.15 = (bf16[2,128,384]{2,1,0:T(8,128)(2,1)S(1)}, bf16[2,128,384]{2,1,0:T(8,128)(2,1)S(1)}, u32[]{:S(2)}, u32[]{:S(2)}) collective-permute-start(bf16[2,128,384]{2,1,0:T(8,128)(2,1)S(1)} %get-tuple-element.41.refs_0_), channel_id=1, source_target_pairs={{0,8},{1,9},{2,10},{3,11},{4,12},{5,13},{6,14},{7,15},{8,0},{9,1},... | collective-permute-start | bytes 589832 | tf_op jit(solution)/shard_map/ppermute | solution.py:47
  95.1 10.7 %collective-permute-start.14 = (bf16[2,128,384]{2,1,0:T(8,128)(2,1)S(1)}, bf16[2,128,384]{2,1,0:T(8,128)(2,1)S(1)}, u32[]{:S(2)}, u32[]{:S(2)}) collective-permute-start(bf16[2,128,384]{2,1,0:T(8,128)(2,1)S(1)} %get-tuple-element.41.refs_0_), channel_id=1, source_target_pairs={{0,4},{1,5},{2,6},{3,7},{4,8},{5,9},{6,10},{7,11},{8,12},{9,13},{1... | collective-permute-start | bytes 589832 | tf_op jit(solution)/shard_map/ppermute | solution.py:47
  96.4 9.4 %collective-permute-start.17 = (bf16[2,128,384]{2,1,0:T(8,128)(2,1)S(1)}, bf16[2,128,384]{2,1,0:T(8,128)(2,1)S(1)}, u32[]{:S(2)}, u32[]{:S(2)}) collective-permute-start(bf16[2,128,384]{2,1,0:T(8,128)(2,1)S(1)} %get-tuple-element.41.refs_0_), channel_id=1, source_target_pairs={{0,1},{1,0},{2,3},{3,2},{4,5},{5,4},{6,7},{7,6},{8,9},{9,8},{10,11... | collective-permute-start | bytes 589832 | tf_op jit(solution)/shard_map/ppermute | solution.py:39
  102.1 3.7 %collective-permute-start.20 = (bf16[2,128,384]{2,1,0:T(8,128)(2,1)S(1)}, bf16[2,128,384]{2,1,0:T(8,128)(2,1)S(1)}, u32[]{:S(2)}, u32[]{:S(2)}) collective-permute-start(bf16[2,128,384]{2,1,0:T(8,128)(2,1)S(1)} %collective-permute-done.16.refs_3_), channel_id=1, source_target_pairs={{0,1},{1,0},{2,3},{3,2},{4,5},{5,4},{6,7},{7,6},{8,9},{9,8},{10,11... | collective-permute-start | bytes 589832 | tf_op jit(solution)/shard_map/ppermute | solution.py:39
  103.7 2.1 %collective-permute-start.19 = (bf16[2,128,384]{2,1,0:T(8,128)(2,1)S(1)}, bf16[2,128,384]{2,1,0:T(8,128)(2,1)S(1)}, u32[]{:S(2)}, u32[]{:S(2)}) collective-permute-start(bf16[2,128,384]{2,1,0:T(8,128)(2,1)S(1)} %collective-permute-done.15.refs_2_), channel_id=1, source_target_pairs={{0,1},{1,0},{2,3},{3,2},{4,5},{5,4},{6,7},{7,6},{8,9},{9,8},{10,11... | collective-permute-start | bytes 589832 | tf_op jit(solution)/shard_map/ppermute | solution.py:39
  148.4 1.6 collective-permute-start.21
  150.8 12.4 %all-to-all-start.5 = ((f32[8,64,128]{2,1,0:T(8,128)}), f32[8,64,128]{2,1,0:T(8,128)S(1)}, u32[]{:S(2)}, u32[]{:S(2)}) async-start(f32[8,64,128]{2,1,0:T(8,128)} %add.3), calls=%async_computation.5 | async-start | bytes 524288 | tf_op jit(solution)/shard_map/all_to_all | solution.py:35
  (17 other events, 92.2 us)

commit v3 on v2

--- a/solution.py
+++ b/solution.py
@@ -47,8 +47,12 @@
     return lax.ppermute(blocks, "col", pairs)
 
 
+def gather_chips(pair):
+    return [pair] + [to_chip(pair, dx, 0) for dx in range(1, 4)]
+
+
 def gather_src(pair):
-    pairs = [pair] + [to_chip(pair, dx, 0) for dx in range(1, 4)]
+    pairs = gather_chips(pair)
     return pairs, [swap_cores(p) for p in pairs]
 
 
@@ -116,15 +120,6 @@
     return slice(128 * block, 128 * block + 128)
 
 
-def series_of(packed):
-    return jnp.concatenate([packed[b, 0:128, :] for b in range(GROUP)], axis=0)
-
-
-def src_of(packed):
-    pieces = [packed[:, 128:160, 0:128], packed[:, 128:160, 128:256]]
-    return side_by_side(jnp.concatenate(pieces, axis=1))
-
-
 def mixing(weight):
     size, chan = 384, weight.shape[0]
     place = lax.broadcasted_iota(jnp.int32, (size, chan), 0) % chan
@@ -133,13 +128,6 @@
     rows = lax.broadcasted_iota(jnp.int32, (size, size), 0) // chan
     cols = lax.broadcasted_iota(jnp.int32, (size, size), 1) // chan
     return jnp.where(rows == cols, tiled, 0.0).astype(BF16)
-
-
-def source_kernel(src_ref, series_ref, src_out):
-    src_out[0:128, :] = series_ref[...]
-    src_out[128:160, 0:128] = src_ref[0:32, :]
-    src_out[128:160, 128:256] = src_ref[32:64, :]
-    src_out[128:160, 256:384] = jnp.zeros((32, 128), BF16)
 
 
 def prepare_kernel(
@@ -174,7 +162,7 @@
         state[...] = jnp.zeros_like(state)
         dst[...] = side_by_side(dst_ref[:, 384:448, :])
 
-    lifted = jnp.maximum(dot_tn(src_of(pick(own_ref, other_ref)), dst[...]), 0.0)
+    lifted = jnp.maximum(dot_tn(side_by_side(pick(own_ref, other_ref)), dst[...]), 0.0)
     old = state[0:1, :]
     new = jnp.maximum(old, jnp.max(lifted, axis=0, keepdims=True))
     total = jnp.sum(jnp.exp(lifted - new), axis=0, keepdims=True)
@@ -201,7 +189,8 @@
 
 
 def hops_kernel(
-    own_ref, other_ref, dst_ref, stats_ref, norm_ref, hop_ref, own_out, other_out, total, dst, second
+    own_ref, other_ref, series_own, series_other, dst_ref, stats_ref,
+    norm_ref, hop_ref, own_out, other_out, total, dst, second,
 ):
     @at_step(0)
     def _():
@@ -216,12 +205,12 @@
         second[...] = side_by_side(dst_ref[:, 0:384, :])
         dst[...] = side_by_side(dst_ref[:, 384:448, :])
 
-    packed = pick(own_ref, other_ref)
-    adjacency = weights_of(src_of(packed), dst[...], norm_ref)[1].astype(BF16)
+    src = side_by_side(pick(own_ref, other_ref))
+    adjacency = weights_of(src, dst[...], norm_ref)[1].astype(BF16)
     carried = dot_nt(second[...], adjacency).astype(BF16)
     for block in range(GROUP):
         put(own_out, other_out, block, carried[:, nodes(block)])
-    accumulate(total, dot_tn(series_of(packed), adjacency))
+    accumulate(total, dot_tn(pick(series_own, series_other), adjacency))
 
     @at_step(1)
     def _():
@@ -229,12 +218,12 @@
             hop_ref[block] = total[:, nodes(block)].astype(BF16)
 
 
-def first_hops(own, other, dst, stats):
-    rows = dst.shape[0] * 128
+def first_hops(*ins):
+    rows = GROUP * 128
     outs = [array(2, rows, dtype=F32)] + [array(GROUP, 384, 128)] * 3
     scratch = [pltpu.VMEM((384, rows), F32), pltpu.VMEM((64, rows), BF16), pltpu.VMEM((384, rows), BF16)]
     size = 2 * rows * rows
-    return call(hops_kernel, 2, (own, other, dst, stats), outs, scratch, 2 * 832 * size, size)
+    return call(hops_kernel, 2, ins, outs, scratch, 2 * 832 * size, size)
 
 
 def sum_of(pack_ref, start, stop):
@@ -282,8 +271,13 @@
         refs[-1][256 * place : 256 * place + 256, :] = ref[...].reshape(256, 384)
 
 
+def after_kernel(first_ref, *refs):
+    del first_ref
+    pieces_kernel(*refs)
+
+
 def grad_kernel(
-    own_ref, other_ref, hop_ref, dst_ref, norm_ref, first_ref,
+    own_ref, other_ref, series_own, series_other, hop_ref, dst_ref, norm_ref, first_ref,
     pack_ref, shift_ref, own_out, other_out, inner, mass, above, below, dst, grads, adj, wide, second,
 ):
     step = pl.program_id(0)
@@ -295,14 +289,14 @@
         grads[0:384, :] = side_by_side(dst_ref[:, 0:384, :])
         grads[384:768, :] = side_by_side(first_ref)
 
-    packed = jnp.where(half == 0, own_ref[...], other_ref[...])
-    src = src_of(packed)
+    src = side_by_side(jnp.where(half == 0, own_ref[...], other_ref[...]))
 
     @pl.when(step < 2)
     def _():
         scores, weights = weights_of(src, dst[...], norm_ref)
         hop = hop_ref[...]
-        adj_grad = dot_nn(jnp.concatenate([hop, series_of(packed)], axis=1), grads[...])
+        series = jnp.where(half == 0, series_own[...], series_other[...])
+        adj_grad = dot_nn(jnp.concatenate([hop, series], axis=1), grads[...])
         adj[half] = adj_grad
         wide[half] = jnp.where(scores > 0.0, weights, 0.0)
         hop_part = dot_tn(hop, weights.astype(BF16))
@@ -370,7 +364,7 @@
 
     size = 2 * rows * rows
     return call(
-        grad_kernel, 4, ins, outs, scratch, 2 * 1408 * size, size, kinds={2: first_pass}, vmem=46 * MIB
+        grad_kernel, 4, ins, outs, scratch, 2 * 1408 * size, size, kinds={4: first_pass}, vmem=46 * MIB
     )
 
 
@@ -390,7 +384,7 @@
             change = shift_ref[:, nodes(block)] - inner[block : block + 1, :]
             scaled[:, nodes(block)] = (dst[:, nodes(block)].astype(F32) * change).astype(BF16)
 
-    scores, weights = weights_of(src_of(pick(own_ref, other_ref)), dst[...], norm_ref)
+    scores, weights = weights_of(side_by_side(pick(own_ref, other_ref)), dst[...], norm_ref)
     part = dot_nt(scaled[...], jnp.where(scores > 0.0, weights, 0.0).astype(BF16))
 
     me = lax.axis_index("col")
@@ -432,13 +426,17 @@
 
 
 def local(dst_embed, src_embed, series, w_self, w_hop1, w_hop2, cotangent):
-    src = call(source_kernel, 1, (src_embed.T, series), [array(160, 384)], vmem=60 * MIB)[0]
+    src = src_embed.T
     src_own, src_other = (jnp.concatenate(p) for p in gather_src(jnp.stack([src, to_chip(src, 0, 1)])))
+    pieces = gather_chips(jnp.stack([series, to_chip(series, 0, 1)]))
     dst, first_mixed, base, mix1, mix2 = prepare(dst_embed.T, series, w_self, w_hop1, w_hop2, cotangent)
     dst = exchange_dst(dst)
-    stats = exchange_dst(softmax_stats(src_own, src_other, dst))
-
-    norm, hop, own, other = first_hops(src_own, src_other, dst, stats)
+    stats = softmax_stats(src_own, src_other, dst)
+    series_own = call(after_kernel, 1, (stats, *pieces), [array(GROUP * 128, 384)])[0]
+    series_other = swap_cores(series_own)
+    stats = exchange_dst(stats)
+
+    norm, hop, own, other = first_hops(src_own, src_other, series_own, series_other, dst, stats)
     hop = exchange_dst(hop)
     pairs = call(cores_kernel, 1, (own, swap_cores(other)), [array(2, 384, 128)] * 4)
     pairs = [pairs[0]] + [to_chip(pairs[dx], -dx, 0) for dx in range(1, 4)]
@@ -454,7 +452,9 @@
     hop_own, hop_other = gather_src(hop_pair)
     hop_all = call(pieces_kernel, 1, (*hop_own, *hop_other), [array(2 * GROUP * 128, 384)])[0]
 
-    pack, shift, own, other = embed_grads(src_own, src_other, hop_all, dst, norm, first)
+    pack, shift, own, other = embed_grads(
+        src_own, src_other, series_own, series_other, hop_all, dst, norm, first
+    )
     pack = exchange_dst(pack)
     own, other = src_grads(src_own, src_other, dst, norm, pack, shift, own, other)
     output, d_dst = call(

time: 164 us -> 166 us (1.012)
  starting transfers between devices: 34.7 us -> 40.4 us
  local copies, waits for them, and re-layouts: 7.25 us -> 5.59 us
    ppermute x12 -> x16, starting transfers between devices: 16.5 us -> 20.7 us  [to_chip(): return lax.ppermute(blocks, 'col', pairs)]
    all_to_all x1, starting transfers between devices: 3.52 us -> 5.65 us  [exchange_src(): return lax.all_to_all(blocks, 'col', 0, 0, axis_index_groups=SAME_CORE)]
    ppermute x12 -> x16, waiting for transfers between devices: 29.3 us -> 27.7 us  [to_chip(): return lax.ppermute(blocks, 'col', pairs)]
    ppermute x10 -> x11, waiting for transfers between devices: 4.27 us -> 4.09 us  [swap_cores(): return lax.ppermute(blocks, 'col', OTHER_CORE)]
  transfers between devices with their start and end apart: 26 -> 31, of which waited for: 13 -> 17; matrix products, arithmetic and copies ran while one was open for 0% -> 0% of each run, Pallas kernels for 4% -> 6%
where the time goes in v3:
time: 166 us; the launch traced here: 165 us
  waiting for transfers between devices  48.5 us (29%)
  starting transfers between devices  40.4 us (24%)
  Pallas kernels  34.1 us (21%)
  blocking collectives  33.8 us (20%)
  local copies, waits for them, and re-layouts  5.59 us (3%)
    pallas_call x11, Pallas kernels, call(): pl.pallas_call(kernel, grid=(steps,), in_specs=specs[:len(ins)], out_spec...  34.1 us
    all_to_all x2, blocking collectives, exchange_dst(): return lax.all_to_all(blocks, 'row', 0, 0)  33.8 us
    ppermute x16, waiting for transfers between devices, to_chip(): return lax.ppermute(blocks, 'col', pairs)  27.7 us
    ppermute x16, starting transfers between devices, to_chip(): return lax.ppermute(blocks, 'col', pairs)  20.7 us
    all_to_all x3, starting transfers between devices, exchange_dst(): return lax.all_to_all(blocks, 'row', 0, 0)  13.8 us
    all_to_all x3, waiting for transfers between devices, exchange_dst(): return lax.all_to_all(blocks, 'row', 0, 0)  9 us
    all_to_all x1, waiting for transfers between devices, exchange_src(): return lax.all_to_all(blocks, 'col', 0, 0, axis_index_groups=SAME_CORE)  7.76 us
    all_to_all x1, starting transfers between devices, exchange_src(): return lax.all_to_all(blocks, 'col', 0, 0, axis_index_groups=SAME_CORE)  5.65 us
  transfers between devices with their start and end apart: 31, of which 17 were waited for; matrix products, arithmetic and copies ran while one was open for 0% of the time, Pallas kernels for 6%

profile of v3, /device:TPU:0, one launch (start us, length us, event | category | flops | bytes accessed | tf_op | source)
XLA Modules:
  0.0 164.8 jit_solution(88579471079079548)
XLA Ops:
  0.6 4.0 %collective-permute-start = (bf16[64,128]{1,0:T(8,128)(2,1)}, bf16[64,128]{1,0:T(8,128)(2,1)S(1)}, u32[]{:S(2)}, u32[]{:S(2)}) collective-permute-start(bf16[64,128]{1,0:T(8,128)(2,1)} %bitcast.13), channel_id=1, source_target_pairs={{0,2},{1,3},{2,0},{3,1},{4,6},{5,7},{6,4},{7,5},{8,10},{9,11},{10,... | collective-permute-start | bytes 49160 | tf_op jit(solution)/shard_map/ppermute | solution.py:47
  4.8 3.3 %shard_map.94 = (bf16[8,448,128]{2,1,0:T(8,128)(2,1)}, f32[384,128]{1,0:T(8,128)}, f32[128,384]{1,0:T(8,128)}, bf16[384,384]{1,0:T(8,128)(2,1)}, bf16[384,384]{1,0:T(8,128)(2,1)}) custom-call(bf16[64,128]{1,0:T(8,128)(2,1)} %bitcast.18, bf16[128,384]{1,0:T(8,128)(2,1)} %series_ref.1, bf16[32,32]{1,0:T(8,128)(2,1)} %self_ref.1, bf16[32,32]{1,0:T(8,128)(2,1)} %hop1_ref.1, ...), custom_call_target="tpu_custom_call" | custom-call | flops 113246208 | bytes 2119680 | tf_op jit(solution)/shard_map/pallas_call | solution.py:75
  8.0 5.5 %all-to-all-start = ((bf16[8,448,128]{2,1,0:T(8,128)(2,1)}), bf16[8,448,128]{2,1,0:T(8,128)(2,1)S(1)}, u32[]{:S(2)}, u32[]{:S(2)}) async-start(bf16[8,448,128]{2,1,0:T(8,128)(2,1)} %get-tuple-element.29), calls=%async_computation | async-start | bytes 1835008 | tf_op jit(solution)/shard_map/all_to_all | solution.py:31
  13.7 2.8 %collective-permute-start.3 = (bf16[2,64,128]{2,1,0:T(8,128)(2,1)S(1)}, bf16[2,64,128]{2,1,0:T(8,128)(2,1)S(1)}, u32[]{:S(2)}, u32[]{:S(2)}) collective-permute-start(bf16[2,64,128]{2,1,0:T(8,128)(2,1)S(1)} %pad_maximum_fusion.1), channel_id=1, source_target_pairs={{0,12},{1,13},{2,14},{3,15},{4,0},{5,1},{6,2},{7,3},{8,4},{9,5},{1... | collective-permute-start | bytes 98312 | tf_op jit(solution)/shard_map/ppermute | solution.py:47
  18.2 3.7 %collective-permute-done.2 = bf16[2,64,128]{2,1,0:T(8,128)(2,1)S(1)} collective-permute-done((bf16[2,64,128]{2,1,0:T(8,128)(2,1)S(1)}, bf16[2,64,128]{2,1,0:T(8,128)(2,1)S(1)}, u32[]{:S(2)}, u32[]{:S(2)}) %collective-permute-start.2) | collective-permute-done | bytes 32800 | tf_op jit(solution)/shard_map/ppermute | solution.py:47
  27.3 3.0 %shard_map.95.first_ref = f32[8,2,1024]{2,1,0:T(2,128)S(1)} custom-call(bf16[8,64,128]{2,1,0:T(8,128)(2,1)S(1)} %constant_dynamic-update-slice_fusion.own_ref, bf16[8,64,128]{2,1,0:T(8,128)(2,1)S(1)} %constant_dynamic-update-slice_fusion.5.other_ref, bf16[8,448,128]{2,1,0:T(8,128)(2,1)S(1)} %all-to-all-done.dst_ref), custom_call_target="tpu_custom_call" | custom-call | flops 268435456 | bytes 1245184 | tf_op jit(solution)/shard_map/pallas_call | solution.py:75
  31.5 2.0 %collective-permute-done.10.refs_2_ = bf16[2,128,384]{2,1,0:T(8,128)(2,1)S(1)} collective-permute-done((bf16[2,128,384]{2,1,0:T(8,128)(2,1)S(1)}, bf16[2,128,384]{2,1,0:T(8,128)(2,1)S(1)}, u32[]{:S(2)}, u32[]{:S(2)}) %collective-permute-start.10) | collective-permute-done | bytes 196640 | tf_op jit(solution)/shard_map/ppermute | solution.py:47
  33.6 3.3 %collective-permute-done.9.refs_1_ = bf16[2,128,384]{2,1,0:T(8,128)(2,1)S(1)} collective-permute-done((bf16[2,128,384]{2,1,0:T(8,128)(2,1)S(1)}, bf16[2,128,384]{2,1,0:T(8,128)(2,1)S(1)}, u32[]{:S(2)}, u32[]{:S(2)}) %collective-permute-start.9) | collective-permute-done | bytes 196640 | tf_op jit(solution)/shard_map/ppermute | solution.py:47
  37.0 11.8 %all_to_all.30.stats_ref = f32[8,2,1024]{2,1,0:T(2,128)S(1)} all-to-all(f32[8,2,1024]{2,1,0:T(2,128)S(1)} %shard_map.95.first_ref), channel_id=1, replica_groups=mesh['row'=8,'col'=16] {'row'}, dimensions={0} | all-to-all | bytes 131072 | tf_op jit(solution)/shard_map/all_to_all | solution.py:31
  48.9 7.2 %shard_map.97 = (f32[2,1024]{1,0:T(2,128)S(1)}, bf16[8,384,128]{2,1,0:T(8,128)(2,1)}, bf16[8,384,128]{2,1,0:T(8,128)(2,1)S(1)}, bf16[8,384,128]{2,1,0:T(8,128)(2,1)}) custom-call(bf16[8,64,128]{2,1,0:T(8,128)(2,1)S(1)} %copy-done.9, bf16[8,64,128]{2,1,0:T(8,128)(2,1)S(1)} %constant_dynamic-update-slice_fusion.5.other_ref, ...), custom_call_target="tpu_custom_call" | custom-call | flops 3489660928 | bytes 5185536 | tf_op jit(solution)/shard_map/pallas_call | solution.py:75
  56.1 3.5 %all-to-all-start.2 = ((bf16[8,384,128]{2,1,0:T(8,128)(2,1)}), bf16[8,384,128]{2,1,0:T(8,128)(2,1)S(1)}, u32[]{:S(2)}, u32[]{:S(2)}) async-start(bf16[8,384,128]{2,1,0:T(8,128)(2,1)} %get-tuple-element.31), calls=%async_computation.2 | async-start | bytes 1572864 | tf_op jit(solution)/shard_map/all_to_all | solution.py:31
  59.6 2.0 %shard_map.98 = (bf16[2,384,128]{2,1,0:T(8,128)(2,1)S(1)}, bf16[2,384,128]{2,1,0:T(8,128)(2,1)}, bf16[2,384,128]{2,1,0:T(8,128)(2,1)}, bf16[2,384,128]{2,1,0:T(8,128)(2,1)}) custom-call(bf16[8,384,128]{2,1,0:T(8,128)(2,1)S(1)} %get-tuple-element.32.own_ref, bf16[8,384,128]{2,1,0:T(8,128)(2,1)} %collective-permute-done.13.other_ref), custom_call_target="tpu_custom_call" | custom-call | bytes 2359296 | tf_op jit(solution)/shard_map/pallas_call | solution.py:75
  64.9 8.5 %all-to-all-done.2.hop_ref = bf16[8,384,128]{2,1,0:T(8,128)(2,1)S(1)} async-done(((bf16[8,384,128]{2,1,0:T(8,128)(2,1)}), bf16[8,384,128]{2,1,0:T(8,128)(2,1)S(1)}, u32[]{:S(2)}, u32[]{:S(2)}) %all-to-all-start.2) | async-done | bytes 786464 | tf_op jit(solution)/shard_map/all_to_all | solution.py:31
  73.4 2.6 %collective-permute-done.16.d_ref = bf16[2,384,128]{2,1,0:T(8,128)(2,1)S(1)} collective-permute-done((bf16[2,384,128]{2,1,0:T(8,128)(2,1)}, bf16[2,384,128]{2,1,0:T(8,128)(2,1)S(1)}, u32[]{:S(2)}, u32[]{:S(2)}) %collective-permute-start.16) | collective-permute-done | bytes 196640 | tf_op jit(solution)/shard_map/ppermute | solution.py:47
  77.2 3.7 %collective-permute-start.17 = (bf16[384,128]{1,0:T(8,128)(2,1)S(1)}, bf16[384,128]{1,0:T(8,128)(2,1)S(1)}, u32[]{:S(2)}, u32[]{:S(2)}) collective-permute-start(bf16[384,128]{1,0:T(8,128)(2,1)S(1)} %get-tuple-element.39), channel_id=1, source_target_pairs={{0,2},{1,3},{2,0},{3,1},{4,6},{5,7},{6,4},{7,5},{8,10},{9,11},{10,... | collective-permute-start | bytes 294920 | tf_op jit(solution)/shard_map/ppermute | solution.py:47
  81.1 2.9 %collective-permute-done.17.other_ref = bf16[384,128]{1,0:T(8,128)(2,1)S(1)} collective-permute-done((bf16[384,128]{1,0:T(8,128)(2,1)S(1)}, bf16[384,128]{1,0:T(8,128)(2,1)S(1)}, u32[]{:S(2)}, u32[]{:S(2)}) %collective-permute-start.17) | collective-permute-done | bytes 98336 | tf_op jit(solution)/shard_map/ppermute | solution.py:47
  84.0 2.9 %collective-permute-done.18.next_ref = bf16[128,384]{1,0:T(8,128)(2,1)S(1)} collective-permute-done((bf16[128,384]{1,0:T(8,128)(2,1)S(1)}, bf16[128,384]{1,0:T(8,128)(2,1)S(1)}, u32[]{:S(2)}, u32[]{:S(2)}) %collective-permute-start.18) | collective-permute-done | bytes 98336 | tf_op jit(solution)/shard_map/ppermute | solution.py:47
  88.9 4.7 %all-to-all-start.3 = ((bf16[8,384,128]{2,1,0:T(8,128)(2,1)}), bf16[8,384,128]{2,1,0:T(8,128)(2,1)}, u32[]{:S(2)}, u32[]{:S(2)}) async-start(bf16[8,384,128]{2,1,0:T(8,128)(2,1)} %get-tuple-element.43), calls=%async_computation.3 | async-start | bytes 1572864 | tf_op jit(solution)/shard_map/all_to_all | solution.py:31
  96.1 4.7 %collective-permute-done.21.refs_3_ = bf16[2,128,384]{2,1,0:T(8,128)(2,1)S(1)} collective-permute-done((bf16[2,128,384]{2,1,0:T(8,128)(2,1)S(1)}, bf16[2,128,384]{2,1,0:T(8,128)(2,1)S(1)}, u32[]{:S(2)}, u32[]{:S(2)}) %collective-permute-start.21) | collective-permute-done | bytes 196640 | tf_op jit(solution)/shard_map/ppermute | solution.py:47
  109.1 12.6 %shard_map.102 = (bf16[8,544,128]{2,1,0:T(8,128)(2,1)S(1)}, f32[1,1024]{1,0:T(1,128)S(1)}, f32[8,64,128]{2,1,0:T(8,128)S(1)}, f32[8,64,128]{2,1,0:T(8,128)S(1)}) custom-call(bf16[8,64,128]{2,1,0:T(8,128)(2,1)S(1)} %copy-done.10, bf16[8,64,128]{2,1,0:T(8,128)(2,1)S(1)} %constant_dynamic-update-slice_fusion.5.other_ref, ...), custom_call_target="tpu_custom_call" | custom-call | flops 5905580032 | bytes 6762496 | tf_op jit(solution)/shard_map/pallas_call | solution.py:75
  121.7 21.9 %all_to_all.31.pack_ref = bf16[8,544,128]{2,1,0:T(8,128)(2,1)S(1)} all-to-all(bf16[8,544,128]{2,1,0:T(8,128)(2,1)S(1)} %get-tuple-element.44), channel_id=1, replica_groups=mesh['row'=8,'col'=16] {'row'}, dimensions={0} | all-to-all | bytes 2228224 | tf_op jit(solution)/shard_map/all_to_all | solution.py:31
  143.7 3.6 %shard_map.104 = (f32[8,64,128]{2,1,0:T(8,128)S(1)}, f32[8,64,128]{2,1,0:T(8,128)S(1)}) custom-call(bf16[8,64,128]{2,1,0:T(8,128)(2,1)S(1)} %copy-done.10, bf16[8,64,128]{2,1,0:T(8,128)(2,1)S(1)} %constant_dynamic-update-slice_fusion.5.other_ref, bf16[8,448,128]{2,1,0:T(8,128)(2,1)S(1)} %all-to-all-done.dst_ref, f32[2,1024]{1,0:T(2,128)S(1)} %get-tuple-element.42.norm_ref, ...), custom_call_target="tpu_custom_call" | custom-call | flops 536870912 | bytes 3354624 | tf_op jit(solution)/shard_map/pallas_call | solution.py:75
  149.7 5.7 %all-to-all-start.5 = ((f32[8,64,128]{2,1,0:T(8,128)}), f32[8,64,128]{2,1,0:T(8,128)S(1)}, u32[]{:S(2)}, u32[]{:S(2)}) async-start(f32[8,64,128]{2,1,0:T(8,128)} %add.3), calls=%async_computation.5 | async-start | bytes 524288 | tf_op jit(solution)/shard_map/all_to_all | solution.py:35
  156.4 7.8 %all-to-all-done.5 = f32[8,64,128]{2,1,0:T(8,128)S(1)} async-done(((f32[8,64,128]{2,1,0:T(8,128)}), f32[8,64,128]{2,1,0:T(8,128)S(1)}, u32[]{:S(2)}, u32[]{:S(2)}) %all-to-all-start.5) | async-done | bytes 262176 | tf_op jit(solution)/shard_map/all_to_all | solution.py:35
  (94 shorter events, 29.9 us)
Async XLA Ops:
  0.6 12.9 %collective-permute-start = (bf16[64,128]{1,0:T(8,128)(2,1)}, bf16[64,128]{1,0:T(8,128)(2,1)S(1)}, u32[]{:S(2)}, u32[]{:S(2)}) collective-permute-start(bf16[64,128]{1,0:T(8,128)(2,1)} %bitcast.13), channel_id=1, source_target_pairs={{0,2},{1,3},{2,0},{3,1},{4,6},{5,7},{6,4},{7,5},{8,10},{9,11},{10,... | collective-permute-start | bytes 49160 | tf_op jit(solution)/shard_map/ppermute | solution.py:47
  4.7 19.0 %collective-permute-start.8 = (bf16[128,384]{1,0:T(8,128)(2,1)}, bf16[128,384]{1,0:T(8,128)(2,1)S(1)}, u32[]{:S(2)}, u32[]{:S(2)}) collective-permute-start(bf16[128,384]{1,0:T(8,128)(2,1)} %series_ref.1), channel_id=1, source_target_pairs={{0,2},{1,3},{2,0},{3,1},{4,6},{5,7},{6,4},{7,5},{8,10},{9,11},{10,... | collective-permute-start | bytes 294920 | tf_op jit(solution)/shard_map/ppermute | solution.py:47
  8.0 19.3 %all-to-all-start = ((bf16[8,448,128]{2,1,0:T(8,128)(2,1)}), bf16[8,448,128]{2,1,0:T(8,128)(2,1)S(1)}, u32[]{:S(2)}, u32[]{:S(2)}) async-start(bf16[8,448,128]{2,1,0:T(8,128)(2,1)} %get-tuple-element.29), calls=%async_computation | async-start | bytes 1835008 | tf_op jit(solution)/shard_map/all_to_all | solution.py:31
  13.6 8.9 %collective-permute-start.4 = (bf16[2,64,128]{2,1,0:T(8,128)(2,1)S(1)}, bf16[2,64,128]{2,1,0:T(8,128)(2,1)S(1)}, u32[]{:S(2)}, u32[]{:S(2)}) collective-permute-start(bf16[2,64,128]{2,1,0:T(8,128)(2,1)S(1)} %pad_maximum_fusion.1), channel_id=1, source_target_pairs={{0,1},{1,0},{2,3},{3,2},{4,5},{5,4},{6,7},{7,6},{8,9},{9,8},{10,11... | collective-permute-start | bytes 98312 | tf_op jit(solution)/shard_map/ppermute | solution.py:39
  16.5 5.4 %collective-permute-start.2 = (bf16[2,64,128]{2,1,0:T(8,128)(2,1)S(1)}, bf16[2,64,128]{2,1,0:T(8,128)(2,1)S(1)}, u32[]{:S(2)}, u32[]{:S(2)}) collective-permute-start(bf16[2,64,128]{2,1,0:T(8,128)(2,1)S(1)} %pad_maximum_fusion.1), channel_id=1, source_target_pairs={{0,8},{1,9},{2,10},{3,11},{4,12},{5,13},{6,14},{7,15},{8,0},{9,1},... | collective-permute-start | bytes 98312 | tf_op jit(solution)/shard_map/ppermute | solution.py:47
  17.3 5.1 %collective-permute-start.1 = (bf16[2,64,128]{2,1,0:T(8,128)(2,1)S(1)}, bf16[2,64,128]{2,1,0:T(8,128)(2,1)S(1)}, u32[]{:S(2)}, u32[]{:S(2)}) collective-permute-start(bf16[2,64,128]{2,1,0:T(8,128)(2,1)S(1)} %pad_maximum_fusion.1), channel_id=1, source_target_pairs={{0,4},{1,5},{2,6},{3,7},{4,8},{5,9},{6,10},{7,11},{8,12},{9,13},{1... | collective-permute-start | bytes 98312 | tf_op jit(solution)/shard_map/ppermute | solution.py:47
  18.2 8.5 %collective-permute-start.7 = (bf16[2,64,128]{2,1,0:T(8,128)(2,1)S(1)}, bf16[2,64,128]{2,1,0:T(8,128)(2,1)S(1)}, u32[]{:S(2)}, u32[]{:S(2)}) collective-permute-start(bf16[2,64,128]{2,1,0:T(8,128)(2,1)S(1)} %collective-permute-done.3), channel_id=1, source_target_pairs={{0,1},{1,0},{2,3},{3,2},{4,5},{5,4},{6,7},{7,6},{8,9},{9,8},{10,11... | collective-permute-start | bytes 98312 | tf_op jit(solution)/shard_map/ppermute | solution.py:39
  21.9 4.8 %collective-permute-start.6 = (bf16[2,64,128]{2,1,0:T(8,128)(2,1)S(1)}, bf16[2,64,128]{2,1,0:T(8,128)(2,1)S(1)}, u32[]{:S(2)}, u32[]{:S(2)}) collective-permute-start(bf16[2,64,128]{2,1,0:T(8,128)(2,1)S(1)} %collective-permute-done.2), channel_id=1, source_target_pairs={{0,1},{1,0},{2,3},{3,2},{4,5},{5,4},{6,7},{7,6},{8,9},{9,8},{10,11... | collective-permute-start | bytes 98312 | tf_op jit(solution)/shard_map/ppermute | solution.py:39
  23.7 7.8 %collective-permute-start.11 = (bf16[2,128,384]{2,1,0:T(8,128)(2,1)S(1)}, bf16[2,128,384]{2,1,0:T(8,128)(2,1)S(1)}, u32[]{:S(2)}, u32[]{:S(2)}) collective-permute-start(bf16[2,128,384]{2,1,0:T(8,128)(2,1)S(1)} %pad_maximum_fusion.refs_0_), channel_id=1, source_target_pairs={{0,12},{1,13},{2,14},{3,15},{4,0},{5,1},{6,2},{7,3},{8,4},{9,5},{1... | collective-permute-start | bytes 589832 | tf_op jit(solution)/shard_map/ppermute | solution.py:47
  24.3 9.3 %collective-permute-start.10 = (bf16[2,128,384]{2,1,0:T(8,128)(2,1)S(1)}, bf16[2,128,384]{2,1,0:T(8,128)(2,1)S(1)}, u32[]{:S(2)}, u32[]{:S(2)}) collective-permute-start(bf16[2,128,384]{2,1,0:T(8,128)(2,1)S(1)} %pad_maximum_fusion.refs_0_), channel_id=1, source_target_pairs={{0,8},{1,9},{2,10},{3,11},{4,12},{5,13},{6,14},{7,15},{8,0},{9,1},... | collective-permute-start | bytes 589832 | tf_op jit(solution)/shard_map/ppermute | solution.py:47
  25.5 11.3 %collective-permute-start.9 = (bf16[2,128,384]{2,1,0:T(8,128)(2,1)S(1)}, bf16[2,128,384]{2,1,0:T(8,128)(2,1)S(1)}, u32[]{:S(2)}, u32[]{:S(2)}) collective-permute-start(bf16[2,128,384]{2,1,0:T(8,128)(2,1)S(1)} %pad_maximum_fusion.refs_0_), channel_id=1, source_target_pairs={{0,4},{1,5},{2,6},{3,7},{4,8},{5,9},{6,10},{7,11},{8,12},{9,13},{1... | collective-permute-start | bytes 589832 | tf_op jit(solution)/shard_map/ppermute | solution.py:47
  36.9 11.9 %collective-permute-start.12 = (bf16[1024,384]{1,0:T(8,128)(2,1)S(1)}, bf16[1024,384]{1,0:T(8,128)(2,1)S(1)}, u32[]{:S(2)}, u32[]{:S(2)}) collective-permute-start(bf16[1024,384]{1,0:T(8,128)(2,1)S(1)} %shard_map.96.series_own), channel_id=1, source_target_pairs={{0,1},{1,0},{2,3},{3,2},{4,5},{5,4},{6,7},{7,6},{8,9},{9,8},{10,11... | collective-permute-start | bytes 2359304 | tf_op jit(solution)/shard_map/ppermute | solution.py:39
  56.1 17.3 %all-to-all-start.2 = ((bf16[8,384,128]{2,1,0:T(8,128)(2,1)}), bf16[8,384,128]{2,1,0:T(8,128)(2,1)S(1)}, u32[]{:S(2)}, u32[]{:S(2)}) async-start(bf16[8,384,128]{2,1,0:T(8,128)(2,1)} %get-tuple-element.31), calls=%async_computation.2 | async-start | bytes 1572864 | tf_op jit(solution)/shard_map/all_to_all | solution.py:31
  62.3 11.1 %collective-permute-start.14 = (bf16[2,384,128]{2,1,0:T(8,128)(2,1)}, bf16[2,384,128]{2,1,0:T(8,128)(2,1)S(1)}, u32[]{:S(2)}, u32[]{:S(2)}) collective-permute-start(bf16[2,384,128]{2,1,0:T(8,128)(2,1)} %get-tuple-element.35), channel_id=1, source_target_pairs={{0,12},{1,13},{2,14},{3,15},{4,0},{5,1},{6,2},{7,3},{8,4},{9,5},{1... | collective-permute-start | bytes 589832 | tf_op jit(solution)/shard_map/ppermute | solution.py:47
  63.1 10.3 %collective-permute-start.15 = (bf16[2,384,128]{2,1,0:T(8,128)(2,1)}, bf16[2,384,128]{2,1,0:T(8,128)(2,1)S(1)}, u32[]{:S(2)}, u32[]{:S(2)}) collective-permute-start(bf16[2,384,128]{2,1,0:T(8,128)(2,1)} %get-tuple-element.36), channel_id=1, source_target_pairs={{0,8},{1,9},{2,10},{3,11},{4,12},{5,13},{6,14},{7,15},{8,0},{9,1},... | collective-permute-start | bytes 589832 | tf_op jit(solution)/shard_map/ppermute | solution.py:47
  64.1 11.9 %collective-permute-start.16 = (bf16[2,384,128]{2,1,0:T(8,128)(2,1)}, bf16[2,384,128]{2,1,0:T(8,128)(2,1)S(1)}, u32[]{:S(2)}, u32[]{:S(2)}) collective-permute-start(bf16[2,384,128]{2,1,0:T(8,128)(2,1)} %get-tuple-element.37), channel_id=1, source_target_pairs={{0,4},{1,5},{2,6},{3,7},{4,8},{5,9},{6,10},{7,11},{8,12},{9,13},{1... | collective-permute-start | bytes 589832 | tf_op jit(solution)/shard_map/ppermute | solution.py:47
  77.2 6.8 %collective-permute-start.17 = (bf16[384,128]{1,0:T(8,128)(2,1)S(1)}, bf16[384,128]{1,0:T(8,128)(2,1)S(1)}, u32[]{:S(2)}, u32[]{:S(2)}) collective-permute-start(bf16[384,128]{1,0:T(8,128)(2,1)S(1)} %get-tuple-element.39), channel_id=1, source_target_pairs={{0,2},{1,3},{2,0},{3,1},{4,6},{5,7},{6,4},{7,5},{8,10},{9,11},{10,... | collective-permute-start | bytes 294920 | tf_op jit(solution)/shard_map/ppermute | solution.py:47
  80.9 6.1 %collective-permute-start.18 = (bf16[128,384]{1,0:T(8,128)(2,1)S(1)}, bf16[128,384]{1,0:T(8,128)(2,1)S(1)}, u32[]{:S(2)}, u32[]{:S(2)}) collective-permute-start(bf16[128,384]{1,0:T(8,128)(2,1)S(1)} %get-tuple-element.40.hop_ref), channel_id=1, source_target_pairs={{0,2},{1,3},{2,0},{3,1},{4,6},{5,7},{6,4},{7,5},{8,10},{9,11},{10,... | collective-permute-start | bytes 294920 | tf_op jit(solution)/shard_map/ppermute | solution.py:47
  88.9 18.2 %all-to-all-start.3 = ((bf16[8,384,128]{2,1,0:T(8,128)(2,1)}), bf16[8,384,128]{2,1,0:T(8,128)(2,1)}, u32[]{:S(2)}, u32[]{:S(2)}) async-start(bf16[8,384,128]{2,1,0:T(8,128)(2,1)} %get-tuple-element.43), calls=%async_computation.3 | async-start | bytes 1572864 | tf_op jit(solution)/shard_map/all_to_all | solution.py:31
  93.6 7.2 %collective-permute-start.21 = (bf16[2,128,384]{2,1,0:T(8,128)(2,1)S(1)}, bf16[2,128,384]{2,1,0:T(8,128)(2,1)S(1)}, u32[]{:S(2)}, u32[]{:S(2)}) collective-permute-start(bf16[2,128,384]{2,1,0:T(8,128)(2,1)S(1)} %get-tuple-element.41.refs_0_), channel_id=1, source_target_pairs={{0,12},{1,13},{2,14},{3,15},{4,0},{5,1},{6,2},{7,3},{8,4},{9,5},{1... | collective-permute-start | bytes 589832 | tf_op jit(solution)/shard_map/ppermute | solution.py:47
  94.3 8.2 %collective-permute-start.20 = (bf16[2,128,384]{2,1,0:T(8,128)(2,1)S(1)}, bf16[2,128,384]{2,1,0:T(8,128)(2,1)S(1)}, u32[]{:S(2)}, u32[]{:S(2)}) collective-permute-start(bf16[2,128,384]{2,1,0:T(8,128)(2,1)S(1)} %get-tuple-element.41.refs_0_), channel_id=1, source_target_pairs={{0,8},{1,9},{2,10},{3,11},{4,12},{5,13},{6,14},{7,15},{8,0},{9,1},... | collective-permute-start | bytes 589832 | tf_op jit(solution)/shard_map/ppermute | solution.py:47
  95.3 9.3 %collective-permute-start.19 = (bf16[2,128,384]{2,1,0:T(8,128)(2,1)S(1)}, bf16[2,128,384]{2,1,0:T(8,128)(2,1)S(1)}, u32[]{:S(2)}, u32[]{:S(2)}) collective-permute-start(bf16[2,128,384]{2,1,0:T(8,128)(2,1)S(1)} %get-tuple-element.41.refs_0_), channel_id=1, source_target_pairs={{0,4},{1,5},{2,6},{3,7},{4,8},{5,9},{6,10},{7,11},{8,12},{9,13},{1... | collective-permute-start | bytes 589832 | tf_op jit(solution)/shard_map/ppermute | solution.py:47
  96.1 8.5 %collective-permute-start.22 = (bf16[2,128,384]{2,1,0:T(8,128)(2,1)S(1)}, bf16[2,128,384]{2,1,0:T(8,128)(2,1)S(1)}, u32[]{:S(2)}, u32[]{:S(2)}) collective-permute-start(bf16[2,128,384]{2,1,0:T(8,128)(2,1)S(1)} %get-tuple-element.41.refs_0_), channel_id=1, source_target_pairs={{0,1},{1,0},{2,3},{3,2},{4,5},{5,4},{6,7},{7,6},{8,9},{9,8},{10,11... | collective-permute-start | bytes 589832 | tf_op jit(solution)/shard_map/ppermute | solution.py:39
  149.7 14.4 %all-to-all-start.5 = ((f32[8,64,128]{2,1,0:T(8,128)}), f32[8,64,128]{2,1,0:T(8,128)S(1)}, u32[]{:S(2)}, u32[]{:S(2)}) async-start(f32[8,64,128]{2,1,0:T(8,128)} %add.3), calls=%async_computation.5 | async-start | bytes 524288 | tf_op jit(solution)/shard_map/all_to_all | solution.py:35
  (22 other events, 120.1 us)

commit v4 on v0

--- a/solution.py
+++ b/solution.py
@@ -11,7 +11,6 @@
 MIB = 1024 * 1024
 VMEM_BYTES = 28 * MIB
 
-SAME_CORE = [[2 * chip + core for chip in range(8)] for core in range(2)]
 OTHER_CORE = [(i, i ^ 1) for i in range(16)]
 
 
@@ -31,8 +30,8 @@
     return lax.all_to_all(blocks, "row", 0, 0)
 
 
-def exchange_src(blocks):
-    return lax.all_to_all(blocks, "col", 0, 0, axis_index_groups=SAME_CORE)
+def exchange_col(blocks):
+    return lax.all_to_all(blocks, "col", 0, 0)
 
 
 def swap_cores(blocks):
@@ -370,7 +369,7 @@
 
 
 def src_kernel(
-    own_ref, other_ref, dst_ref, norm_ref, pack_ref, shift_ref, own_part, other_part, own_out, other_out, scaled, dst
+    own_ref, other_ref, dst_ref, norm_ref, pack_ref, shift_ref, own_part, other_part, out_ref, scaled, dst
 ):
     @at_step(0)
     def _():
@@ -389,19 +388,19 @@
 
         @at_step(0)
         def _(block=block, place=place):
-            own_out[place] = own_part[block] + part[:, nodes(block)]
+            out_ref[place * 2 + me % 2] = (own_part[block] + part[:, nodes(block)]).astype(BF16)
 
         @at_step(1)
         def _(block=block, place=place):
-            other_out[place] = other_part[block] + part[:, nodes(block)]
+            out_ref[place * 2 + 1 - me % 2] = (other_part[block] + part[:, nodes(block)]).astype(BF16)
 
 
 def src_grads(*ins):
     rows = ins[2].shape[0] * 128
-    outs = [array(GROUP, 64, 128, dtype=F32), array(GROUP, 64, 128, dtype=F32)]
+    outs = [array(2 * GROUP, 64, 128)]
     scratch = [pltpu.VMEM((64, rows), BF16), pltpu.VMEM((64, rows), BF16)]
     size = 2 * rows * rows
-    return call(src_kernel, 2, ins, outs, scratch, 256 * size, size)
+    return call(src_kernel, 2, ins, outs, scratch, 256 * size, size)[0]
 
 
 def output_kernel(pack_ref, hop_ref, base_ref, mix1_ref, mix2_ref, out_ref, d_dst_ref):
@@ -442,12 +441,12 @@
 
     pack, shift, own, other = embed_grads(src_own, src_other, hop_own, hop_other, dst, norm, first)
     pack = exchange_dst(pack)
-    own, other = src_grads(src_own, src_other, dst, norm, pack, shift, own, other)
+    d_src = src_grads(src_own, src_other, dst, norm, pack, shift, own, other)
     output, d_dst = call(
         output_kernel, 1, (pack, hop, base, mix1, mix2), [array(128, 384), array(64, 128, dtype=F32)],
         flops=4 * 128 * 384 * 384,
     )
-    d_src = jnp.sum(exchange_src(own + swap_cores(other)), axis=0)
+    d_src = jnp.sum(exchange_col(d_src).astype(F32), axis=0)
     return output, d_dst.T, d_src.T
 
 

time: 163 us -> 163 us (level)
  waiting for transfers between devices: 43.6 us -> 40.7 us
  local copies, waits for them, and re-layouts: 10.6 us -> 12.5 us
    unnamed x35, local copies, waits for them, and re-layouts: 8.91 us -> 10.8 us
  transfers between devices with their start and end apart: 26 -> 25, of which waited for: 11 -> 10; matrix products, arithmetic and copies ran while one was open for 5% -> 5% of each run, Pallas kernels for 4% -> 4%
where the time goes in v4:
time: 163 us; the launch traced here: 161 us
  waiting for transfers between devices  40.7 us (25%)
  Pallas kernels  37.8 us (23%)
  starting transfers between devices  35.6 us (22%)
  blocking collectives  32 us (20%)
  local copies, waits for them, and re-layouts  12.5 us (8%)
  other arithmetic  1.75 us (1%)
    pallas_call x10, Pallas kernels, call(): pl.pallas_call(kernel, grid=(steps,), in_specs=specs[:len(ins)], out_spec...  37.8 us
    all_to_all x2, blocking collectives, exchange_dst(): return lax.all_to_all(blocks, 'row', 0, 0)  32 us
    ppermute x12, waiting for transfers between devices, to_chip(): return lax.ppermute(blocks, 'col', pairs)  22.6 us
    ppermute x12, starting transfers between devices, to_chip(): return lax.ppermute(blocks, 'col', pairs)  16.5 us
    all_to_all x3, starting transfers between devices, exchange_dst(): return lax.all_to_all(blocks, 'row', 0, 0)  14.1 us
    unnamed x35, local copies, waits for them, and re-layouts  10.8 us
    all_to_all x3, waiting for transfers between devices, exchange_dst(): return lax.all_to_all(blocks, 'row', 0, 0)  10.4 us
    all_to_all x1, waiting for transfers between devices, exchange_col(): return lax.all_to_all(blocks, 'col', 0, 0)  6.32 us
  transfers between devices with their start and end apart: 25, of which 10 were waited for; matrix products, arithmetic and copies ran while one was open for 5% of the time, Pallas kernels for 4%

profile of v4, /device:TPU:0, one launch (start us, length us, event | category | flops | bytes accessed | tf_op | source)
XLA Modules:
  0.0 161.3 jit_solution(9988045944090682979)
XLA Ops:
  2.2 4.0 %collective-permute-start = (bf16[160,384]{1,0:T(8,128)(2,1)}, bf16[160,384]{1,0:T(8,128)(2,1)S(1)}, u32[]{:S(2)}, u32[]{:S(2)}) collective-permute-start(bf16[160,384]{1,0:T(8,128)(2,1)} %shard_map.94), channel_id=1, source_target_pairs={{0,2},{1,3},{2,0},{3,1},{4,6},{5,7},{6,4},{7,5},{8,10},{9,11},{10,... | collective-permute-start | bytes 368648 | tf_op jit(solution)/shard_map/ppermute | solution.py:46
  6.2 3.3 %shard_map.95 = (bf16[8,448,128]{2,1,0:T(8,128)(2,1)}, f32[384,128]{1,0:T(8,128)}, f32[128,384]{1,0:T(8,128)}, bf16[384,384]{1,0:T(8,128)(2,1)}, bf16[384,384]{1,0:T(8,128)(2,1)}) custom-call(bf16[64,128]{1,0:T(8,128)(2,1)} %bitcast.22, bf16[128,384]{1,0:T(8,128)(2,1)} %series_ref.3, bf16[32,32]{1,0:T(8,128)(2,1)} %self_ref.1, bf16[32,32]{1,0:T(8,128)(2,1)} %hop1_ref.1, ...), custom_call_target="tpu_custom_call" | custom-call | flops 113246208 | bytes 2119680 | tf_op jit(solution)/shard_map/pallas_call | solution.py:71
  9.4 4.9 %all-to-all-start = ((bf16[8,448,128]{2,1,0:T(8,128)(2,1)}), bf16[8,448,128]{2,1,0:T(8,128)(2,1)S(1)}, u32[]{:S(2)}, u32[]{:S(2)}) async-start(bf16[8,448,128]{2,1,0:T(8,128)(2,1)} %get-tuple-element.25), calls=%async_computation | async-start | bytes 1835008 | tf_op jit(solution)/shard_map/all_to_all | solution.py:30
  14.5 2.8 %collective-permute-start.3 = (bf16[2,160,384]{2,1,0:T(8,128)(2,1)S(1)}, bf16[2,160,384]{2,1,0:T(8,128)(2,1)S(1)}, u32[]{:S(2)}, u32[]{:S(2)}) collective-permute-start(bf16[2,160,384]{2,1,0:T(8,128)(2,1)S(1)} %pad_maximum_fusion.1), channel_id=1, source_target_pairs={{0,12},{1,13},{2,14},{3,15},{4,0},{5,1},{6,2},{7,3},{8,4},{9,5},{1... | collective-permute-start | bytes 737288 | tf_op jit(solution)/shard_map/ppermute | solution.py:46
  19.1 9.4 %collective-permute-done.3 = bf16[2,160,384]{2,1,0:T(8,128)(2,1)S(1)} collective-permute-done((bf16[2,160,384]{2,1,0:T(8,128)(2,1)S(1)}, bf16[2,160,384]{2,1,0:T(8,128)(2,1)S(1)}, u32[]{:S(2)}, u32[]{:S(2)}) %collective-permute-start.3) | collective-permute-done | bytes 245792 | tf_op jit(solution)/shard_map/ppermute | solution.py:46
  29.0 3.2 %collective-permute-done.1 = bf16[2,160,384]{2,1,0:T(8,128)(2,1)S(1)} collective-permute-done((bf16[2,160,384]{2,1,0:T(8,128)(2,1)S(1)}, bf16[2,160,384]{2,1,0:T(8,128)(2,1)S(1)}, u32[]{:S(2)}, u32[]{:S(2)}) %collective-permute-start.1) | collective-permute-done | bytes 245792 | tf_op jit(solution)/shard_map/ppermute | solution.py:46
  33.8 3.0 %shard_map.96 = f32[8,2,1024]{2,1,0:T(2,128)S(1)} custom-call(bf16[8,160,384]{2,1,0:T(8,128)(2,1)S(1)} %constant_dynamic-update-slice_fusion.own_ref, bf16[8,160,384]{2,1,0:T(8,128)(2,1)S(1)} %constant_dynamic-update-slice_fusion.5.other_ref, bf16[8,448,128]{2,1,0:T(8,128)(2,1)S(1)} %all-to-all-done.dst_ref), custom_call_target="tpu_custom_call" | custom-call | flops 268435456 | bytes 2949120 | tf_op jit(solution)/shard_map/pallas_call | solution.py:71
  36.9 11.8 %all_to_all.30.stats_ref = f32[8,2,1024]{2,1,0:T(2,128)S(1)} all-to-all(f32[8,2,1024]{2,1,0:T(2,128)S(1)} %shard_map.96), channel_id=1, replica_groups=mesh['row'=8,'col'=16] {'row'}, dimensions={0} | all-to-all | bytes 131072 | tf_op jit(solution)/shard_map/all_to_all | solution.py:30
  48.7 7.2 %shard_map.97 = (f32[2,1024]{1,0:T(2,128)S(1)}, bf16[8,384,128]{2,1,0:T(8,128)(2,1)S(1)}, bf16[8,384,128]{2,1,0:T(8,128)(2,1)S(1)}, bf16[8,384,128]{2,1,0:T(8,128)(2,1)}) custom-call(bf16[8,160,384]{2,1,0:T(8,128)(2,1)S(1)} %constant_dynamic-update-slice_fusion.own_ref, bf16[8,160,384]{2,1,0:T(8,128)(2,1)S(1)} %constant_dynamic-update-slice_fusion.5.other_ref, ...), custom_call_target="tpu_custom_call" | custom-call | flops 3489660928 | bytes 5316608 | tf_op jit(solution)/shard_map/pallas_call | solution.py:71
  57.6 3.5 %all-to-all-start.2 = ((bf16[8,384,128]{2,1,0:T(8,128)(2,1)}), bf16[8,384,128]{2,1,0:T(8,128)(2,1)S(1)}, u32[]{:S(2)}, u32[]{:S(2)}) async-start(bf16[8,384,128]{2,1,0:T(8,128)(2,1)} %copy-done.3), calls=%async_computation.2 | async-start | bytes 1572864 | tf_op jit(solution)/shard_map/all_to_all | solution.py:30
  62.3 2.0 %shard_map.98 = (bf16[2,384,128]{2,1,0:T(8,128)(2,1)S(1)}, bf16[2,384,128]{2,1,0:T(8,128)(2,1)}, bf16[2,384,128]{2,1,0:T(8,128)(2,1)}, bf16[2,384,128]{2,1,0:T(8,128)(2,1)}) custom-call(bf16[8,384,128]{2,1,0:T(8,128)(2,1)S(1)} %copy-done.5, bf16[8,384,128]{2,1,0:T(8,128)(2,1)} %collective-permute-done.8.other_ref), custom_call_target="tpu_custom_call" | custom-call | bytes 2359296 | tf_op jit(solution)/shard_map/pallas_call | solution.py:71
  66.6 8.4 %all-to-all-done.2.hop_ref = bf16[8,384,128]{2,1,0:T(8,128)(2,1)S(1)} async-done(((bf16[8,384,128]{2,1,0:T(8,128)(2,1)}), bf16[8,384,128]{2,1,0:T(8,128)(2,1)S(1)}, u32[]{:S(2)}, u32[]{:S(2)}) %all-to-all-start.2) | async-done | bytes 786464 | tf_op jit(solution)/shard_map/all_to_all | solution.py:30
  75.0 3.1 %collective-permute-done.11.d_ref = bf16[2,384,128]{2,1,0:T(8,128)(2,1)} collective-permute-done((bf16[2,384,128]{2,1,0:T(8,128)(2,1)}, bf16[2,384,128]{2,1,0:T(8,128)(2,1)}, u32[]{:S(2)}, u32[]{:S(2)}) %collective-permute-start.11) | collective-permute-done | bytes 196640 | tf_op jit(solution)/shard_map/ppermute | solution.py:46
  81.3 2.4 %collective-permute-start.20 = (bf16[384,128]{1,0:T(8,128)(2,1)S(1)}, bf16[384,128]{1,0:T(8,128)(2,1)S(1)}, u32[]{:S(2)}, u32[]{:S(2)}) collective-permute-start(bf16[384,128]{1,0:T(8,128)(2,1)S(1)} %get-tuple-element.37), channel_id=1, source_target_pairs={{0,2},{1,3},{2,0},{3,1},{4,6},{5,7},{6,4},{7,5},{8,10},{9,11},{10,... | collective-permute-start | bytes 294920 | tf_op jit(solution)/shard_map/ppermute | solution.py:46
  83.7 2.7 %collective-permute-done.12 = bf16[128,384]{1,0:T(8,128)(2,1)S(1)} collective-permute-done((bf16[128,384]{1,0:T(8,128)(2,1)S(1)}, bf16[128,384]{1,0:T(8,128)(2,1)S(1)}, u32[]{:S(2)}, u32[]{:S(2)}) %collective-permute-start.12) | collective-permute-done | bytes 98336 | tf_op jit(solution)/shard_map/ppermute | solution.py:46
  89.7 5.6 %all-to-all-start.3 = ((bf16[8,384,128]{2,1,0:T(8,128)(2,1)}), bf16[8,384,128]{2,1,0:T(8,128)(2,1)}, u32[]{:S(2)}, u32[]{:S(2)}) async-start(bf16[8,384,128]{2,1,0:T(8,128)(2,1)} %shard_map.100), calls=%async_computation.3 | async-start | bytes 1572864 | tf_op jit(solution)/shard_map/all_to_all | solution.py:30
  96.8 3.4 %collective-permute-done.13 = bf16[2,128,384]{2,1,0:T(8,128)(2,1)} collective-permute-done((bf16[2,128,384]{2,1,0:T(8,128)(2,1)S(1)}, bf16[2,128,384]{2,1,0:T(8,128)(2,1)}, u32[]{:S(2)}, u32[]{:S(2)}) %collective-permute-start.13) | collective-permute-done | bytes 196640 | tf_op jit(solution)/shard_map/ppermute | solution.py:46
  101.8 1.7 %constant_dynamic-update-slice_fusion.10 = bf16[8,128,384]{2,1,0:T(8,128)(2,1)} fusion(bf16[8,128,384]{2,1,0:T(8,128)(2,1)} %constant_dynamic-update-slice_fusion.11, bf16[2,128,384]{2,1,0:T(8,128)(2,1)} %collective-permute-done.14), kind=kLoop, calls=%fused_computation.14 | loop fusion | bytes 393216
  106.2 2.0 %all-to-all-done.3.first_ref = bf16[8,384,128]{2,1,0:T(8,128)(2,1)} async-done(((bf16[8,384,128]{2,1,0:T(8,128)(2,1)}), bf16[8,384,128]{2,1,0:T(8,128)(2,1)}, u32[]{:S(2)}, u32[]{:S(2)}) %all-to-all-start.3) | async-done | bytes 786464 | tf_op jit(solution)/shard_map/all_to_all | solution.py:30
  109.4 13.2 %shard_map.101 = (bf16[8,544,128]{2,1,0:T(8,128)(2,1)S(1)}, f32[1,1024]{1,0:T(1,128)S(1)}, f32[8,64,128]{2,1,0:T(8,128)S(1)}, f32[8,64,128]{2,1,0:T(8,128)S(1)}) custom-call(bf16[8,160,384]{2,1,0:T(8,128)(2,1)S(1)} %copy-done.1, bf16[8,160,384]{2,1,0:T(8,128)(2,1)S(1)} %constant_dynamic-update-slice_fusion.5.other_ref, ...), custom_call_target="tpu_custom_call" | custom-call | flops 5905580032 | bytes 6893568 | tf_op jit(solution)/shard_map/pallas_call | solution.py:71
  122.6 20.2 %all_to_all.31.pack_ref = bf16[8,544,128]{2,1,0:T(8,128)(2,1)S(1)} all-to-all(bf16[8,544,128]{2,1,0:T(8,128)(2,1)S(1)} %get-tuple-element.38), channel_id=1, replica_groups=mesh['row'=8,'col'=16] {'row'}, dimensions={0} | all-to-all | bytes 2228224 | tf_op jit(solution)/shard_map/all_to_all | solution.py:30
  142.8 4.3 %shard_map.103 = bf16[16,64,128]{2,1,0:T(8,128)(2,1)} custom-call(bf16[8,160,384]{2,1,0:T(8,128)(2,1)S(1)} %copy-done.2, bf16[8,160,384]{2,1,0:T(8,128)(2,1)S(1)} %constant_dynamic-update-slice_fusion.5.other_ref, bf16[8,448,128]{2,1,0:T(8,128)(2,1)S(1)} %all-to-all-done.dst_ref, f32[2,1024]{1,0:T(2,128)S(1)} %get-tuple-element.34.norm_ref, ...), custom_call_target="tpu_custom_call" | custom-call | flops 536870912 | bytes 4796416 | tf_op jit(solution)/shard_map/pallas_call | solution.py:71
  147.1 4.3 %all-to-all-start.5 = ((bf16[16,64,128]{2,1,0:T(8,128)(2,1)}), bf16[16,64,128]{2,1,0:T(8,128)(2,1)S(1)}, u32[]{:S(2)}, u32[]{:S(2)}) async-start(bf16[16,64,128]{2,1,0:T(8,128)(2,1)} %shard_map.103), calls=%async_computation.5 | async-start | bytes 524288 | tf_op jit(solution)/shard_map/all_to_all | solution.py:34
  154.3 6.3 %all-to-all-done.5 = bf16[16,64,128]{2,1,0:T(8,128)(2,1)S(1)} async-done(((bf16[16,64,128]{2,1,0:T(8,128)(2,1)}), bf16[16,64,128]{2,1,0:T(8,128)(2,1)S(1)}, u32[]{:S(2)}, u32[]{:S(2)}) %all-to-all-start.5) | async-done | bytes 262176 | tf_op jit(solution)/shard_map/all_to_all | solution.py:34
  (80 shorter events, 27.6 us)
Async XLA Ops:
  2.2 12.2 %collective-permute-start = (bf16[160,384]{1,0:T(8,128)(2,1)}, bf16[160,384]{1,0:T(8,128)(2,1)S(1)}, u32[]{:S(2)}, u32[]{:S(2)}) collective-permute-start(bf16[160,384]{1,0:T(8,128)(2,1)} %shard_map.94), channel_id=1, source_target_pairs={{0,2},{1,3},{2,0},{3,1},{4,6},{5,7},{6,4},{7,5},{8,10},{9,11},{10,... | collective-permute-start | bytes 368648 | tf_op jit(solution)/shard_map/ppermute | solution.py:46
  9.4 24.4 %all-to-all-start = ((bf16[8,448,128]{2,1,0:T(8,128)(2,1)}), bf16[8,448,128]{2,1,0:T(8,128)(2,1)S(1)}, u32[]{:S(2)}, u32[]{:S(2)}) async-start(bf16[8,448,128]{2,1,0:T(8,128)(2,1)} %get-tuple-element.25), calls=%async_computation | async-start | bytes 1835008 | tf_op jit(solution)/shard_map/all_to_all | solution.py:30
  14.4 17.7 %collective-permute-start.4 = (bf16[2,160,384]{2,1,0:T(8,128)(2,1)S(1)}, bf16[2,160,384]{2,1,0:T(8,128)(2,1)S(1)}, u32[]{:S(2)}, u32[]{:S(2)}) collective-permute-start(bf16[2,160,384]{2,1,0:T(8,128)(2,1)S(1)} %pad_maximum_fusion.1), channel_id=1, source_target_pairs={{0,1},{1,0},{2,3},{3,2},{4,5},{5,4},{6,7},{7,6},{8,9},{9,8},{10,11... | collective-permute-start | bytes 737288 | tf_op jit(solution)/shard_map/ppermute | solution.py:38
  14.5 13.9 %collective-permute-start.3 = (bf16[2,160,384]{2,1,0:T(8,128)(2,1)S(1)}, bf16[2,160,384]{2,1,0:T(8,128)(2,1)S(1)}, u32[]{:S(2)}, u32[]{:S(2)}) collective-permute-start(bf16[2,160,384]{2,1,0:T(8,128)(2,1)S(1)} %pad_maximum_fusion.1), channel_id=1, source_target_pairs={{0,12},{1,13},{2,14},{3,15},{4,0},{5,1},{6,2},{7,3},{8,4},{9,5},{1... | collective-permute-start | bytes 737288 | tf_op jit(solution)/shard_map/ppermute | solution.py:46
  17.3 11.1 %collective-permute-start.2 = (bf16[2,160,384]{2,1,0:T(8,128)(2,1)S(1)}, bf16[2,160,384]{2,1,0:T(8,128)(2,1)S(1)}, u32[]{:S(2)}, u32[]{:S(2)}) collective-permute-start(bf16[2,160,384]{2,1,0:T(8,128)(2,1)S(1)} %pad_maximum_fusion.1), channel_id=1, source_target_pairs={{0,8},{1,9},{2,10},{3,11},{4,12},{5,13},{6,14},{7,15},{8,0},{9,1},... | collective-permute-start | bytes 737288 | tf_op jit(solution)/shard_map/ppermute | solution.py:46
  18.1 14.0 %collective-permute-start.1 = (bf16[2,160,384]{2,1,0:T(8,128)(2,1)S(1)}, bf16[2,160,384]{2,1,0:T(8,128)(2,1)S(1)}, u32[]{:S(2)}, u32[]{:S(2)}) collective-permute-start(bf16[2,160,384]{2,1,0:T(8,128)(2,1)S(1)} %pad_maximum_fusion.1), channel_id=1, source_target_pairs={{0,4},{1,5},{2,6},{3,7},{4,8},{5,9},{6,10},{7,11},{8,12},{9,13},{1... | collective-permute-start | bytes 737288 | tf_op jit(solution)/shard_map/ppermute | solution.py:46
  28.5 5.3 %collective-permute-start.7 = (bf16[2,160,384]{2,1,0:T(8,128)(2,1)S(1)}, bf16[2,160,384]{2,1,0:T(8,128)(2,1)S(1)}, u32[]{:S(2)}, u32[]{:S(2)}) collective-permute-start(bf16[2,160,384]{2,1,0:T(8,128)(2,1)S(1)} %collective-permute-done.3), channel_id=1, source_target_pairs={{0,1},{1,0},{2,3},{3,2},{4,5},{5,4},{6,7},{7,6},{8,9},{9,8},{10,11... | collective-permute-start | bytes 737288 | tf_op jit(solution)/shard_map/ppermute | solution.py:38
  28.5 5.2 %collective-permute-start.6 = (bf16[2,160,384]{2,1,0:T(8,128)(2,1)S(1)}, bf16[2,160,384]{2,1,0:T(8,128)(2,1)S(1)}, u32[]{:S(2)}, u32[]{:S(2)}) collective-permute-start(bf16[2,160,384]{2,1,0:T(8,128)(2,1)S(1)} %collective-permute-done.2), channel_id=1, source_target_pairs={{0,1},{1,0},{2,3},{3,2},{4,5},{5,4},{6,7},{7,6},{8,9},{9,8},{10,11... | collective-permute-start | bytes 737288 | tf_op jit(solution)/shard_map/ppermute | solution.py:38
  57.6 3.6 %collective-permute-start.8 = (bf16[8,384,128]{2,1,0:T(8,128)(2,1)}, bf16[8,384,128]{2,1,0:T(8,128)(2,1)}, u32[]{:S(2)}, u32[]{:S(2)}) collective-permute-start(bf16[8,384,128]{2,1,0:T(8,128)(2,1)} %get-tuple-element.28), channel_id=1, source_target_pairs={{0,1},{1,0},{2,3},{3,2},{4,5},{5,4},{6,7},{7,6},{8,9},{9,8},{10,11... | collective-permute-start | bytes 2359304 | tf_op jit(solution)/shard_map/ppermute | solution.py:38
  57.6 17.3 %all-to-all-start.2 = ((bf16[8,384,128]{2,1,0:T(8,128)(2,1)}), bf16[8,384,128]{2,1,0:T(8,128)(2,1)S(1)}, u32[]{:S(2)}, u32[]{:S(2)}) async-start(bf16[8,384,128]{2,1,0:T(8,128)(2,1)} %copy-done.3), calls=%async_computation.2 | async-start | bytes 1572864 | tf_op jit(solution)/shard_map/all_to_all | solution.py:30
  64.4 10.6 %collective-permute-start.9 = (bf16[2,384,128]{2,1,0:T(8,128)(2,1)}, bf16[2,384,128]{2,1,0:T(8,128)(2,1)S(1)}, u32[]{:S(2)}, u32[]{:S(2)}) collective-permute-start(bf16[2,384,128]{2,1,0:T(8,128)(2,1)} %get-tuple-element.30), channel_id=1, source_target_pairs={{0,12},{1,13},{2,14},{3,15},{4,0},{5,1},{6,2},{7,3},{8,4},{9,5},{1... | collective-permute-start | bytes 589832 | tf_op jit(solution)/shard_map/ppermute | solution.py:46
  65.1 9.9 %collective-permute-start.10 = (bf16[2,384,128]{2,1,0:T(8,128)(2,1)}, bf16[2,384,128]{2,1,0:T(8,128)(2,1)}, u32[]{:S(2)}, u32[]{:S(2)}) collective-permute-start(bf16[2,384,128]{2,1,0:T(8,128)(2,1)} %get-tuple-element.31), channel_id=1, source_target_pairs={{0,8},{1,9},{2,10},{3,11},{4,12},{5,13},{6,14},{7,15},{8,0},{9,1},... | collective-permute-start | bytes 589832 | tf_op jit(solution)/shard_map/ppermute | solution.py:46
  65.8 12.4 %collective-permute-start.11 = (bf16[2,384,128]{2,1,0:T(8,128)(2,1)}, bf16[2,384,128]{2,1,0:T(8,128)(2,1)}, u32[]{:S(2)}, u32[]{:S(2)}) collective-permute-start(bf16[2,384,128]{2,1,0:T(8,128)(2,1)} %get-tuple-element.32), channel_id=1, source_target_pairs={{0,4},{1,5},{2,6},{3,7},{4,8},{5,9},{6,10},{7,11},{8,12},{9,13},{1... | collective-permute-start | bytes 589832 | tf_op jit(solution)/shard_map/ppermute | solution.py:46
  79.5 7.0 %collective-permute-start.12 = (bf16[128,384]{1,0:T(8,128)(2,1)S(1)}, bf16[128,384]{1,0:T(8,128)(2,1)S(1)}, u32[]{:S(2)}, u32[]{:S(2)}) collective-permute-start(bf16[128,384]{1,0:T(8,128)(2,1)S(1)} %get-tuple-element.33.hop_ref), channel_id=1, source_target_pairs={{0,2},{1,3},{2,0},{3,1},{4,6},{5,7},{6,4},{7,5},{8,10},{9,11},{10,... | collective-permute-start | bytes 294920 | tf_op jit(solution)/shard_map/ppermute | solution.py:46
  81.3 7.4 %collective-permute-start.20 = (bf16[384,128]{1,0:T(8,128)(2,1)S(1)}, bf16[384,128]{1,0:T(8,128)(2,1)S(1)}, u32[]{:S(2)}, u32[]{:S(2)}) collective-permute-start(bf16[384,128]{1,0:T(8,128)(2,1)S(1)} %get-tuple-element.37), channel_id=1, source_target_pairs={{0,2},{1,3},{2,0},{3,1},{4,6},{5,7},{6,4},{7,5},{8,10},{9,11},{10,... | collective-permute-start | bytes 294920 | tf_op jit(solution)/shard_map/ppermute | solution.py:46
  86.5 18.7 %collective-permute-start.16 = (bf16[2,128,384]{2,1,0:T(8,128)(2,1)S(1)}, bf16[2,128,384]{2,1,0:T(8,128)(2,1)S(1)}, u32[]{:S(2)}, u32[]{:S(2)}) collective-permute-start(bf16[2,128,384]{2,1,0:T(8,128)(2,1)S(1)} %pad_maximum_fusion.2), channel_id=1, source_target_pairs={{0,1},{1,0},{2,3},{3,2},{4,5},{5,4},{6,7},{7,6},{8,9},{9,8},{10,11... | collective-permute-start | bytes 589832 | tf_op jit(solution)/shard_map/ppermute | solution.py:38
  86.6 9.4 %collective-permute-start.15 = (bf16[2,128,384]{2,1,0:T(8,128)(2,1)S(1)}, bf16[2,128,384]{2,1,0:T(8,128)(2,1)}, u32[]{:S(2)}, u32[]{:S(2)}) collective-permute-start(bf16[2,128,384]{2,1,0:T(8,128)(2,1)S(1)} %pad_maximum_fusion.2), channel_id=1, source_target_pairs={{0,12},{1,13},{2,14},{3,15},{4,0},{5,1},{6,2},{7,3},{8,4},{9,5},{1... | collective-permute-start | bytes 589832 | tf_op jit(solution)/shard_map/ppermute | solution.py:46
  87.4 9.4 %collective-permute-start.14 = (bf16[2,128,384]{2,1,0:T(8,128)(2,1)S(1)}, bf16[2,128,384]{2,1,0:T(8,128)(2,1)}, u32[]{:S(2)}, u32[]{:S(2)}) collective-permute-start(bf16[2,128,384]{2,1,0:T(8,128)(2,1)S(1)} %pad_maximum_fusion.2), channel_id=1, source_target_pairs={{0,8},{1,9},{2,10},{3,11},{4,12},{5,13},{6,14},{7,15},{8,0},{9,1},... | collective-permute-start | bytes 589832 | tf_op jit(solution)/shard_map/ppermute | solution.py:46
  88.2 12.0 %collective-permute-start.13 = (bf16[2,128,384]{2,1,0:T(8,128)(2,1)S(1)}, bf16[2,128,384]{2,1,0:T(8,128)(2,1)}, u32[]{:S(2)}, u32[]{:S(2)}) collective-permute-start(bf16[2,128,384]{2,1,0:T(8,128)(2,1)S(1)} %pad_maximum_fusion.2), channel_id=1, source_target_pairs={{0,4},{1,5},{2,6},{3,7},{4,8},{5,9},{6,10},{7,11},{8,12},{9,13},{1... | collective-permute-start | bytes 589832 | tf_op jit(solution)/shard_map/ppermute | solution.py:46
  89.7 18.6 %all-to-all-start.3 = ((bf16[8,384,128]{2,1,0:T(8,128)(2,1)}), bf16[8,384,128]{2,1,0:T(8,128)(2,1)}, u32[]{:S(2)}, u32[]{:S(2)}) async-start(bf16[8,384,128]{2,1,0:T(8,128)(2,1)} %shard_map.100), calls=%async_computation.3 | async-start | bytes 1572864 | tf_op jit(solution)/shard_map/all_to_all | solution.py:30
  96.0 9.2 %collective-permute-start.19 = (bf16[2,128,384]{2,1,0:T(8,128)(2,1)}, bf16[2,128,384]{2,1,0:T(8,128)(2,1)S(1)}, u32[]{:S(2)}, u32[]{:S(2)}) collective-permute-start(bf16[2,128,384]{2,1,0:T(8,128)(2,1)} %collective-permute-done.15), channel_id=1, source_target_pairs={{0,1},{1,0},{2,3},{3,2},{4,5},{5,4},{6,7},{7,6},{8,9},{9,8},{10,11... | collective-permute-start | bytes 589832 | tf_op jit(solution)/shard_map/ppermute | solution.py:38
  96.8 8.4 %collective-permute-start.18 = (bf16[2,128,384]{2,1,0:T(8,128)(2,1)}, bf16[2,128,384]{2,1,0:T(8,128)(2,1)S(1)}, u32[]{:S(2)}, u32[]{:S(2)}) collective-permute-start(bf16[2,128,384]{2,1,0:T(8,128)(2,1)} %collective-permute-done.14), channel_id=1, source_target_pairs={{0,1},{1,0},{2,3},{3,2},{4,5},{5,4},{6,7},{7,6},{8,9},{9,8},{10,11... | collective-permute-start | bytes 589832 | tf_op jit(solution)/shard_map/ppermute | solution.py:38
  100.2 5.0 %collective-permute-start.17 = (bf16[2,128,384]{2,1,0:T(8,128)(2,1)}, bf16[2,128,384]{2,1,0:T(8,128)(2,1)S(1)}, u32[]{:S(2)}, u32[]{:S(2)}) collective-permute-start(bf16[2,128,384]{2,1,0:T(8,128)(2,1)} %collective-permute-done.13), channel_id=1, source_target_pairs={{0,1},{1,0},{2,3},{3,2},{4,5},{5,4},{6,7},{7,6},{8,9},{9,8},{10,11... | collective-permute-start | bytes 589832 | tf_op jit(solution)/shard_map/ppermute | solution.py:38
  147.1 13.5 %all-to-all-start.5 = ((bf16[16,64,128]{2,1,0:T(8,128)(2,1)}), bf16[16,64,128]{2,1,0:T(8,128)(2,1)S(1)}, u32[]{:S(2)}, u32[]{:S(2)}) async-start(bf16[16,64,128]{2,1,0:T(8,128)(2,1)} %shard_map.103), calls=%async_computation.5 | async-start | bytes 524288 | tf_op jit(solution)/shard_map/all_to_all | solution.py:34
  (13 other events, 91.7 us)
